TPU v7x, 128 devices: a whole 4x4x4 slice. The times are simulated.
128 devices in a mesh: row: 8 (over z, x_lo), col: 16 (over x_hi, y, core).
Axes of the slice: x: 4 (x_hi: 2, x_lo: 2; x = x_hi * 2 + x_lo), y: 4, z: 4, core: 2. Of those that a mesh axis runs over, the one named last changes fastest.
Arguments:
- atom_feats: bfloat16 [20480, 128], P(('row', 'col')), may hold values from -6 to 6
- atom_counts: int32 [2048], replicated, may hold values from 1 to 24, as said below
- w_atom: bfloat16 [128, 768], replicated, may hold values from -0.5 to 0.5
- single_in: bfloat16 [2048, 768], P(('row', 'col')), may hold values from -6 to 6
- w_qkv: bfloat16 [3, 768, 768], P(None, None, 'col'), may hold values from -0.21875 to 0.21875
- w_out: bfloat16 [768, 768], P('col'), may hold values from -0.21875 to 0.21875
- pair: bfloat16 [2048, 2048, 128], P('row', 'col'), may hold values from -6 to 6
- w_pair: bfloat16 [128, 16], replicated, may hold values from -0.5 to 0.5
- cotangent: bfloat16 [2048, 768], P(('row', 'col')), may hold values from -192 to 192
Outputs:
- updated: bfloat16 [2048, 768], P(('row', 'col'))
- grad_pair: bfloat16 [2048, 2048, 128], P('row', 'col')
- grad_pair_weight: float32 [128, 16], replicated
Inputs may be any that keep to these rules, and one draw needn't show every extreme that they name: `atom_counts`: atoms of one token are consecutive, tokens in order. Each aligned block of 256 tokens holds exactly 2560 atoms; its first 112 tokens have 19 to 24 atoms, one of them 24, and its last 144 tokens are small-molecule tokens of one atom.
All inputs are finite; a program needn't handle non-finite values.
Results may differ from a plain program's by a relative error of at most 0.025.
Values may be sent and summed in bfloat16 or wider, within the bound.
A program may use at most 64 MiB of HBM per device.

v0:
```python
import jax
import jax.numpy as jnp
from jax import lax
from jax.sharding import PartitionSpec as P

HD = 48


def on_device(atom_feats, atom_counts, w_atom, single_in, w_qkv, w_out, pair, w_pair, cotangent):
    atom_dev = atom_feats.shape[0]
    device = lax.axis_index(("row", "col"))
    row_place = lax.axis_index("row")
    col_count = lax.axis_size("col")
    ends_at = jnp.cumsum(atom_counts)
    counts_f = atom_counts.astype(jnp.float32)
    own_rows = single_in.shape[0]
    block_tokens = own_rows * col_count
    atom_ids = device * atom_dev + jnp.arange(atom_dev, dtype=jnp.int32)
    token_of = jnp.sum((ends_at[None, :] <= atom_ids[:, None]).astype(jnp.int32), axis=1)
    atom_hidden = jax.nn.relu(
        jnp.dot(atom_feats, w_atom, preferred_element_type=jnp.float32)
    ).astype(jnp.bfloat16)
    token_base = row_place * block_tokens
    wanted = token_base + jnp.arange(lax.axis_size("col") * own_rows, dtype=jnp.int32)
    onehot = (token_of[None, :] == wanted[:, None]).astype(jnp.bfloat16)
    summed = jnp.dot(onehot, atom_hidden, preferred_element_type=jnp.float32)
    pooled = lax.psum_scatter(
        (
            summed
            / lax.dynamic_slice_in_dim(counts_f, token_base, lax.axis_size("col") * own_rows)[
                :, None
            ]
        ).astype(jnp.bfloat16),
        "col",
        scatter_dimension=0,
        tiled=True,
    ).astype(jnp.float32)
    single = (single_in.astype(jnp.float32) + pooled).astype(jnp.bfloat16)
    block_rows = lax.all_gather(single, "col", axis=0, tiled=True)
    values32 = block_rows.astype(jnp.float32)
    center = jnp.mean(values32, axis=1, keepdims=True)
    spread = jnp.mean((values32 - center) ** 2, axis=1, keepdims=True)
    normed = ((values32 - center) / jnp.sqrt(spread + 1e-05)).astype(jnp.bfloat16)
    queries = jnp.dot(normed, w_qkv[0], preferred_element_type=jnp.float32).astype(jnp.bfloat16)
    keys_mine = jnp.dot(normed, w_qkv[1], preferred_element_type=jnp.float32).astype(jnp.bfloat16)
    values_mine = jnp.dot(normed, w_qkv[2], preferred_element_type=jnp.float32).astype(jnp.bfloat16)
    keys_all, values_all = (
        lax.all_gather(keys_mine, "row", axis=0, tiled=True),
        lax.all_gather(values_mine, "row", axis=0, tiled=True),
    )
    rows_here = normed.shape[0]
    heads_here = queries.shape[1] // HD
    local_bias = jnp.einsum("ijc,ch->hij", pair, w_pair, preferred_element_type=jnp.float32).astype(
        jnp.bfloat16
    )
    bias_mine = lax.all_to_all(local_bias, "col", split_axis=0, concat_axis=2, tiled=True)
    q_heads = queries.reshape(rows_here, heads_here, HD)
    k_heads = keys_all.reshape(-1, heads_here, HD)
    v_heads = values_all.reshape(-1, heads_here, HD)
    scores = jnp.einsum(
        "ihd,jhd->hij", q_heads, k_heads, preferred_element_type=jnp.float32
    ) / jnp.sqrt(jnp.float32(HD))
    scores = scores + bias_mine.astype(jnp.float32)
    top = jnp.max(scores, axis=2, keepdims=True)
    expd = jnp.exp(scores - top)
    probs = expd / jnp.sum(expd, axis=2, keepdims=True)
    attended = jnp.einsum(
        "hij,jhd->ihd", probs.astype(jnp.bfloat16), v_heads, preferred_element_type=jnp.float32
    )
    attended = attended.astype(jnp.bfloat16).reshape(rows_here, heads_here * HD)
    projected = lax.psum_scatter(
        jnp.dot(attended, w_out, preferred_element_type=jnp.float32).astype(jnp.bfloat16),
        "col",
        scatter_dimension=0,
        tiled=True,
    ).astype(jnp.float32)
    cot_rows = lax.all_gather(cotangent, "col", axis=0, tiled=True)
    d_attended = lax.dot_general(
        cot_rows, w_out, (((1,), (1,)), ((), ())), preferred_element_type=jnp.float32
    ).astype(jnp.bfloat16)
    updated = (single.astype(jnp.float32) + projected).astype(jnp.bfloat16)
    d_heads = d_attended.reshape(rows_here, heads_here, HD)
    d_probs = jnp.einsum("ihd,jhd->hij", d_heads, v_heads, preferred_element_type=jnp.float32)
    inner = jnp.sum(probs * d_probs, axis=2, keepdims=True)
    d_bias = (probs * (d_probs - inner)).astype(jnp.bfloat16)
    d_local = lax.all_to_all(d_bias, "col", split_axis=2, concat_axis=0, tiled=True)
    grad_pair = jnp.einsum(
        "hij,ch->ijc", d_local, w_pair, preferred_element_type=jnp.float32
    ).astype(jnp.bfloat16)
    weight_part = jnp.einsum("ijc,hij->ch", pair, d_local, preferred_element_type=jnp.float32)
    grad_pair_weight = lax.psum(weight_part, ("row", "col"))
    return (updated, grad_pair, grad_pair_weight)


def solution(mesh):
    placed = (
        P(("row", "col"), None),
        P(),
        P(),
        P(("row", "col"), None),
        P(None, None, "col"),
        P("col", None),
        P("row", "col", None),
        P(),
        P(("row", "col"), None),
    )
    return jax.shard_map(
        on_device,
        mesh=mesh,
        in_specs=placed,
        out_specs=(P(("row", "col"), None), P("row", "col", None), P()),
        check_vma=False,
    )
```

profile of v0, /device:TPU:1, one launch (start us, length us, event | category | flops | bytes accessed | tf_op | source)
XLA Modules:
  0.0 352.2 jit_solution(10444828441904062281)
XLA Ops:
  7.2 0.0 copy-start
  7.2 0.0 reduce-scatter.3.cloned.1.call-start
  7.3 0.8 dynamic-slice_convert_fusion
  8.1 1.0 reduce-window.9
  9.0 0.1 slice.21
  9.1 0.1 slice_reduce_fusion
  9.3 0.1 add_bitcast_fusion
  9.3 0.3 convert_reduce_fusion
  9.6 2.0 fusion.3
  11.6 0.0 reduce-scatter.3.cloned.1.call-update
  11.6 5.7 %convolution_convert_fusion.1 = bf16[16,256,128]{2,0,1:T(8,128)(2,1)S(1)} fusion(bf16[256,128,128]{2,1,0:T(8,128)(2,1)} %param.15, bf16[128,16]{0,1:T(8,128)(2,1)S(1)} %copy-done.5), kind=kOutput, calls=%fused_computation.9 | convolution fusion | flops 134742016 | bytes 9441280 | tf_op jit(solution)/shard_map/ijc,ch->hij/dot_general | solution.py:53
  17.3 1.3 copy.16
  18.6 8.6 %all-to-all-start = ((bf16[16,256,128]{2,1,0:T(8,128)(2,1)}), bf16[16,256,128]{2,1,0:T(8,128)(2,1)S(1)}, u32[]{:S(2)}, u32[]{:S(2)}) async-start(bf16[16,256,128]{2,1,0:T(8,128)(2,1)} %copy.16), calls=%async_computation.1 | async-start | bytes 2097152 | tf_op jit(solution)/shard_map/all_to_all | solution.py:56
  27.1 31.7 %all_gather.15 = bf16[256,768]{1,0:T(8,128)(2,1)S(1)} all-gather(bf16[16,768]{1,0:T(8,128)(2,1)S(1)} %copy-done.3), channel_id=1, replica_groups=mesh['row'=8,'col'=16] {'col'}, dimensions={0}, use_global_device_ids=true | all-gather | bytes 417792 | tf_op jit(solution)/shard_map/all_gather | solution.py:77
  58.8 19.6 %reduce-scatter.3.cloned.1.call-done = bf16[16,768]{1,0:T(8,128)(2,1)} async-done(((bf16[256,768]{1,0:T(8,128)(2,1)}), bf16[16,768]{1,0:T(8,128)(2,1)}) %reduce-scatter.3.cloned.1.call-update) | async-done | bytes 24592 | tf_op jit(solution)/shard_map/reduce_scatter | solution.py:27
  78.5 0.7 add_convert_fusion.1
  79.2 25.0 %all_gather.12 = bf16[256,768]{1,0:T(8,128)(2,1)S(1)} all-gather(bf16[16,768]{1,0:T(8,128)(2,1)S(1)} %add_convert_fusion.1), channel_id=1, replica_groups=mesh['row'=8,'col'=16] {'col'}, dimensions={0}, use_global_device_ids=true | all-gather | bytes 417792 | tf_op jit(solution)/shard_map/all_gather | solution.py:39
  104.2 0.1 convert_reduce_fusion.1
  104.3 0.2 fusion.14
  104.6 0.2 fusion.15
  104.8 0.2 convolution_convert_fusion.7
  105.0 24.6 %all_gather.13 = bf16[2048,48]{0,1:T(8,128)(2,1)} all-gather(bf16[256,48]{0,1:T(8,128)(2,1)S(1)} %convolution_convert_fusion.7), channel_id=1, replica_groups=mesh['row'=8,'col'=16] {'row'}, dimensions={0}, use_global_device_ids=true | all-gather | bytes 221184 | tf_op jit(solution)/shard_map/all_gather | solution.py:49
  129.6 0.2 convolution_convert_fusion.5
  129.8 22.6 %all_gather.14 = bf16[2048,48]{0,1:T(8,128)(2,1)S(1)} all-gather(bf16[256,48]{0,1:T(8,128)(2,1)S(1)} %convolution_convert_fusion.5), channel_id=1, replica_groups=mesh['row'=8,'col'=16] {'row'}, dimensions={0}, use_global_device_ids=true | all-gather | bytes 221184 | tf_op jit(solution)/shard_map/all_gather | solution.py:48
  152.4 0.2 convert_bitcast_fusion
  152.7 2.5 copy.17
  155.2 3.0 fusion.33
  158.2 0.4 fusion.2
  158.7 0.5 copy-done.2
  159.2 0.1 copy-done.6
  159.2 2.2 multiply_reduce_fusion
  161.5 2.2 fusion.7
  163.6 3.8 %copy.18 = bf16[1,256,2048]{1,0,2:T(2,128)(2,1)} copy(bf16[1,256,2048]{2,1,0:T(8,128)(2,1)S(1)} %fusion.7) | data formatting | bytes 2097152 | tf_op jit(solution)/shard_map/convert_element_type | solution.py:85
  167.4 0.5 broadcast.52
  167.9 11.6 %reduce.8 = bf16[2048,256]{1,0:T(8,128)(2,1)S(1)} reduce(bf16[2048,1,256]{2,1,0:T(2,128)(2,1)} %bitcast.68, bf16[]{:T(256)} %broadcast.52), dimensions={1}, to_apply=%bitcast.49.reduce_sub_computation | reduce | bytes 2097154
  179.5 1.1 reshape.115
  180.7 16.5 %all-to-all-start.1 = ((bf16[16,2,16384]{2,1,0:T(2,128)(2,1)}), bf16[16,2,16384]{2,1,0:T(2,128)(2,1)S(1)}, u32[]{:S(2)}, u32[]{:S(2)}) async-start(bf16[16,2,16384]{2,1,0:T(2,128)(2,1)} %reshape.115), calls=%async_computation.3 | async-start | bytes 2097152 | tf_op jit(solution)/shard_map/all_to_all | solution.py:86
  197.1 0.2 reduce-scatter.5.cloned.1.call-start
  197.3 2.7 convolution_convert_fusion.2
  200.0 0.0 reduce-scatter.5.cloned.1.call-update
  200.0 66.0 %reduce-scatter.5.cloned.1.call-done = bf16[16,768]{1,0:T(8,128)(2,1)} async-done(((bf16[256,768]{1,0:T(8,128)(2,1)}), bf16[16,768]{1,0:T(8,128)(2,1)}) %reduce-scatter.5.cloned.1.call-update) | async-done | bytes 24592 | tf_op jit(solution)/shard_map/reduce_scatter | solution.py:71
  266.1 1.4 add_convert_fusion
  267.4 1.0 reshape.116
  268.5 0.2 copy.21
  268.7 1.1 copy.20
  269.7 4.6 %convolution_bitcast_fusion = f32[128,16]{0,1:T(8,128)S(1)} fusion(bf16[256,128,128]{2,1,0:T(8,128)(2,1)} %param.15, bf16[1,256,16,128]{3,2,1,0:T(8,128)(2,1)S(1)} %copy.20), kind=kOutput, calls=%fused_computation.23 | convolution fusion | flops 134217728 | bytes 9445376 | tf_op jit(solution)/shard_map/ijc,hij->ch/dot_general | solution.py:90
  274.3 4.7 %convolution_convert_fusion = bf16[256,128,128]{2,1,0:T(8,128)(2,1)} fusion(bf16[1,256,16,128]{3,2,1,0:T(8,128)(2,1)S(1)} %copy.20, bf16[128,16]{0,1:T(8,128)(2,1)S(1)} %copy-done.5), kind=kOutput, calls=%fused_computation | convolution fusion | flops 138412032 | bytes 9441280 | tf_op jit(solution)/shard_map/hij,ch->ijc/dot_general | solution.py:87
  279.1 66.3 %psum.7 = f32[128,16]{0,1:T(8,128)} all-reduce(f32[128,16]{0,1:T(8,128)S(1)} %convolution_bitcast_fusion), channel_id=1, replica_groups=mesh['row'=8,'col'=16] {'row','col'}, use_global_device_ids=true, to_apply=%region_10.11 | all-reduce | flops 2048 | bytes 16384 | tf_op jit(solution)/shard_map/psum | solution.py:91
  (17 shorter events, 0.1 us)
Async XLA Ops:
  7.2 2.5 copy-start
  7.2 4.4 %copy-start.5 = (bf16[128,16]{0,1:T(8,128)(2,1)S(1)}, bf16[128,16]{0,1:T(8,128)(2,1)}, u32[]{:S(2)}) copy-start(bf16[128,16]{0,1:T(8,128)(2,1)} %param.16) | copy-start | bytes 12292
  7.2 71.3 %reduce-scatter.3.cloned.1.call-start = ((), (), s32[]{:S(2)}) async-start(), calls=%async_computation.4 | async-start | bytes 417792 | tf_op jit(solution)/shard_map/reduce_scatter | solution.py:27
  17.3 9.8 %copy-start.3 = (bf16[16,768]{1,0:T(8,128)(2,1)S(1)}, bf16[16,768]{1,0:T(8,128)(2,1)}, u32[]{:S(2)}) copy-start(bf16[16,768]{1,0:T(8,128)(2,1)} %param.17) | copy-start | bytes 73732
  17.3 61.2 %copy-start.4 = (bf16[16,768]{1,0:T(8,128)(2,1)S(1)}, bf16[16,768]{1,0:T(8,128)(2,1)}, u32[]{:S(2)}) copy-start(bf16[16,768]{1,0:T(8,128)(2,1)} %param.12) | copy-start | bytes 73732
  18.6 86.2 %copy-start.1 = (bf16[3,768,48]{1,2,0:T(8,128)(2,1)S(1)}, bf16[3,768,48]{1,2,0:T(8,128)(2,1)}, u32[]{:S(2)}) copy-start(bf16[3,768,48]{1,2,0:T(8,128)(2,1)} %param.13) | copy-start | bytes 663556
  18.6 133.9 %all-to-all-start = ((bf16[16,256,128]{2,1,0:T(8,128)(2,1)}), bf16[16,256,128]{2,1,0:T(8,128)(2,1)S(1)}, u32[]{:S(2)}, u32[]{:S(2)}) async-start(bf16[16,256,128]{2,1,0:T(8,128)(2,1)} %copy.16), calls=%async_computation.1 | async-start | bytes 2097152 | tf_op jit(solution)/shard_map/all_to_all | solution.py:56
  158.2 0.9 copy-start.2
  158.2 1.0 copy-start.6
  180.7 86.8 %all-to-all-start.1 = ((bf16[16,2,16384]{2,1,0:T(2,128)(2,1)}), bf16[16,2,16384]{2,1,0:T(2,128)(2,1)S(1)}, u32[]{:S(2)}, u32[]{:S(2)}) async-start(bf16[16,2,16384]{2,1,0:T(2,128)(2,1)} %reshape.115), calls=%async_computation.3 | async-start | bytes 2097152 | tf_op jit(solution)/shard_map/all_to_all | solution.py:86
  197.1 69.0 %reduce-scatter.5.cloned.1.call-start = ((), (), s32[]{:S(2)}) async-start(), calls=%async_computation.5 | async-start | bytes 417792 | tf_op jit(solution)/shard_map/reduce_scatter | solution.py:71
Sparse Core Ops, SparseCore 0:
  11.8 66.6 reduce-scatter.2
  202.2 63.8 reduce-scatter.4
where the time goes:
time: 353 us; the launch traced here: 352 us
  blocking collectives  170 us (48%)
  waiting for transfers between devices  85.7 us (24%)
  matrix products  25.4 us (7%)
  starting transfers between devices  25.3 us (7%)
  other arithmetic  19.3 us (5%)
  between operations  14.2 us (4%)
  local copies, waits for them, and re-layouts  12.2 us (3%)
    psum x1, blocking collectives, on_device(): grad_pair_weight = lax.psum(weight_part, ('row', 'col'))  66.3 us
    reduce_scatter x1, waiting for transfers between devices, on_device(): lax.psum_scatter(jnp.dot(attended, w_out, preferred_element_type=jnp.floa...  66 us
    all_gather x1, blocking collectives, on_device(): cot_rows = lax.all_gather(cotangent, 'col', axis=0, tiled=True)  31.7 us
    all_gather x1, blocking collectives, on_device(): block_rows = lax.all_gather(single, 'col', axis=0, tiled=True)  25 us
    all_gather x1, blocking collectives, on_device(): lax.all_gather(values_mine, 'row', axis=0, tiled=True)  24.6 us
    all_gather x1, blocking collectives, on_device(): lax.all_gather(keys_mine, 'row', axis=0, tiled=True)  22.6 us
    reduce_scatter x1, waiting for transfers between devices, on_device(): lax.psum_scatter((summed / lax.dynamic_slice_in_dim(counts_f, token_base,...  19.6 us
    all_to_all x1, starting transfers between devices, on_device(): lax.all_to_all(d_bias, 'col', split_axis=2, concat_axis=0, tiled=True)  16.5 us
  transfers between devices with their start and end apart: 4, of which 2 were waited for; matrix products, arithmetic and copies ran while one was open for 4% of the time, Pallas kernels for 0%

commit v1 on v0

v1 whole, which is shorter than its diff:
```python
import functools

import jax
import jax.numpy as jnp
from jax import lax
from jax.experimental import pallas as pl
from jax.experimental.pallas import tpu as pltpu
from jax.sharding import PartitionSpec as P

MESH = pl.DeviceIdType.MESH
BF = jnp.bfloat16
F32 = jnp.float32
NC = 16
NR = 8
HD = 48
D = 768
GT = 16
SCALE = 1.0 / (48.0**0.5)


def nt(a, b):
    return lax.dot_general(a, b, (((1,), (1,)), ((), ())), preferred_element_type=F32)


def nn(a, b):
    return jnp.dot(a, b, preferred_element_type=F32)


def head_tiles():
    return [(h, t) for h in range(NC) for t in range(6) if 48 * h < 128 * t + 128 and 48 * h + 48 > 128 * t]


def spread(rows, mask_ref):
    pairs = set(head_tiles())
    zero = jnp.zeros((GT, 128), BF)
    out = []
    for h in range(NC):
        out.append(
            jnp.concatenate(
                [
                    rows[:, 128 * t : 128 * t + 128] * mask_ref[16 * h : 16 * h + 16, 128 * t : 128 * t + 128]
                    if (h, t) in pairs
                    else zero
                    for t in range(6)
                ],
                axis=1,
            )
        )
    return jnp.concatenate(out, axis=0)


def main_kernel(
    feats, counts, w_atom, single_in, w_qkv, w_out, pair, w_pair, cot,
    d_out, upd_out, wg_out,
    pairv, part, pool_recv, acc, norm_all, cot_all, wo_all, kv_send, kv_all, q_all, da_all,
    wbd, wt, mask, bias, ebuf, dpbuf, st_send, st_recv, fin_all, att_send, att_recv,
    dbuf, dt, wcol, wrow, krow, vrow, qrow, darow, single_v,
    pair_sem, d_sem,
    pool_ss, pool_rs, norm_ss, norm_rs, cot_ss, cot_rs, wo_ss, wo_rs, kv_ss, kv_rs, q_ss, q_rs,
    da_ss, da_rs, st_ss, st_rs, fin_ss, fin_rs, att_ss, att_rs, wc_ss, wc_rs, wr_ss, wr_rs,
):
    r = lax.axis_index("row")
    c = lax.axis_index("col")

    def loop(lo, hi, body):
        def step(k, carry):
            body(k)
            return carry

        lax.fori_loop(lo, hi, step, 0)

    def pair_copy(g):
        return pltpu.make_async_copy(pair.at[pl.ds(g * GT, GT)], pairv.at[pl.ds(g * GT, GT)], pair_sem.at[g])

    loop(0, 16, lambda g: pair_copy(g).start())

    bar = pltpu.get_barrier_semaphore()
    src_row = c // 2

    def greet_col(k):
        pl.semaphore_signal(bar, inc=1, device_id=(r, lax.rem(c + k, NC)), device_id_type=MESH)

    def greet_row(k):
        pl.semaphore_signal(bar, inc=1, device_id=(lax.rem(r + k, NR), c), device_id_type=MESH)

    def greet_kv(h):
        @pl.when(jnp.logical_or(src_row != r, h != c))
        def _():
            pl.semaphore_signal(bar, inc=1, device_id=(src_row, h), device_id_type=MESH)

    loop(1, NC, greet_col)
    loop(1, NR, greet_row)
    loop(0, NC, greet_kv)

    crow = jnp.concatenate([counts[pl.ds(2 * r, 1), :], counts[pl.ds(2 * r + 1, 1), :]], axis=1).astype(F32)
    tok = lax.broadcasted_iota(jnp.int32, (256, 256), 0)
    lan = lax.broadcasted_iota(jnp.int32, (256, 256), 1)
    cbig = jnp.broadcast_to(crow, (256, 256))
    ends = jnp.sum(jnp.where(lan <= tok, cbig, 0.0), axis=1, keepdims=True)
    cnt = jnp.sum(jnp.where(lan == tok, cbig, 0.0), axis=1, keepdims=True)
    atom = (lan + 160 * c).astype(F32)
    inside = jnp.logical_and(jnp.logical_and(atom < ends, atom >= ends - cnt), lan < 160)
    onehot = jnp.where(inside, 1.0, 0.0).astype(BF)
    x = jnp.concatenate([feats[...], jnp.zeros((96, 128), BF)], axis=0)
    hidden = jnp.maximum(nn(x, w_atom[...]), 0.0).astype(BF)
    part[...] = (nn(onehot, hidden) / cnt).astype(BF).reshape(NC, GT, D)

    row16 = lax.broadcasted_iota(jnp.int32, (16, 256), 0)
    lan16 = lax.broadcasted_iota(jnp.int32, (16, 256), 1)
    rep = jnp.where(lan16 // 16 == row16, 1.0, 0.0).astype(BF)
    wrep = nn(w_pair[...], rep)
    lanw = lax.broadcasted_iota(jnp.int32, (128, 256), 1)
    for i in range(GT):
        wbd[128 * i : 128 * i + 128, :] = jnp.where(lax.rem(lanw, 16) == i, wrep, 0.0).astype(BF)
    eye = jnp.where(
        lax.broadcasted_iota(jnp.int32, (48, 48), 0) == lax.broadcasted_iota(jnp.int32, (48, 48), 1), 1.0, 0.0
    ).astype(BF)
    for m in range(3):
        wt[48 * m : 48 * m + 48, :] = nt(eye, w_qkv[m]).astype(BF)
    mrow = lax.broadcasted_iota(jnp.int32, (256, D), 0)
    mlan = lax.broadcasted_iota(jnp.int32, (256, D), 1)
    mask[...] = jnp.where(mlan // 48 == mrow // 16, 1.0, 0.0).astype(BF)
    cot_all[c] = cot[...]
    wo_all[c] = w_out[...]

    pl.semaphore_wait(bar, 38 - jnp.where(src_row == r, 1, 0))

    def lo(s):
        return (160 * s) // 384

    def hi(s):
        return jnp.where(s == 15, 15, jnp.minimum(6, (160 * s + 159) // 304))

    def pool_copy(o, s):
        return pltpu.make_async_remote_copy(
            part.at[o], pool_recv.at[s], pool_ss.at[o], pool_rs.at[s], device_id=(r, o), device_id_type=MESH
        )

    def sends_to(s, o):
        return jnp.logical_and(jnp.logical_and(o >= lo(s), o <= hi(s)), o != s)

    def pool_start(o):
        @pl.when(sends_to(c, o))
        def _():
            pool_copy(o, c).start()

    loop(0, NC, pool_start)

    def gather_copy(buf, ss, rs, peer, slot):
        return pltpu.make_async_remote_copy(
            buf.at[slot], buf.at[slot], ss.at[peer], rs.at[slot], device_id=(r, peer), device_id_type=MESH
        )

    def gather_start(buf, ss, rs):
        def body(k):
            gather_copy(buf, ss, rs, lax.rem(c + k, NC), c).start()

        loop(1, NC, body)

    def gather_wait(buf, ss, rs):
        def body(k):
            p = lax.rem(c + NC - k, NC)
            gather_copy(buf, ss, rs, p, p).wait_recv()

        loop(1, NC, body)

    def gather_sent(buf, ss, rs):
        def body(k):
            gather_copy(buf, ss, rs, lax.rem(c + k, NC), c).wait_send()

        loop(1, NC, body)

    gather_start(cot_all, cot_ss, cot_rs)

    def bias_group(g):
        pair_copy(g).wait()
        lhs = jnp.concatenate([pairv[g * GT + i] for i in range(GT)], axis=1)
        bias[g] = nn(lhs, wbd[...])

    loop(0, 4, bias_group)

    acc[...] = single_in[...].astype(F32) + part[c].astype(F32)

    def pool_take(s):
        @pl.when(sends_to(s, c))
        def _():
            pool_copy(c, s).wait_recv()
            acc[...] += pool_recv[s].astype(F32)

    loop(0, NC, pool_take)
    single = acc[...].astype(BF)
    single_v[...] = single
    v32 = single.astype(F32)
    center = jnp.mean(v32, axis=1, keepdims=True)
    diff = v32 - center
    var = jnp.mean(diff * diff, axis=1, keepdims=True)
    norm_all[c] = (diff / jnp.sqrt(var + 1e-05)).astype(BF)
    gather_start(norm_all, norm_ss, norm_rs)

    loop(4, 9, bias_group)

    gather_wait(cot_all, cot_ss, cot_rs)
    da_all[c] = nt(w_out[...], cot_all[...].reshape(256, D)).astype(BF)
    gather_start(da_all, da_ss, da_rs)

    loop(9, 12, bias_group)

    gather_wait(norm_all, norm_ss, norm_rs)
    qkv = nt(wt[...], norm_all[...].reshape(256, D)).astype(BF)
    q_all[c] = qkv[0:48]
    kv_send[0] = qkv[48:144, 0:128]
    kv_send[1] = qkv[48:144, 128:256]
    gather_start(q_all, q_ss, q_rs)

    def kv_copy(n, src, r2):
        return pltpu.make_async_remote_copy(
            kv_send.at[lax.rem(n, 2)],
            kv_all.at[src],
            kv_ss.at[n],
            kv_rs.at[src],
            device_id=(n // 2, 2 * r2 + lax.rem(n, 2)),
            device_id_type=MESH,
        )

    def is_self(n):
        return jnp.logical_and(n // 2 == r, 2 * r + lax.rem(n, 2) == c)

    def kv_start(k):
        n = lax.rem(k + 2 * r, 16)

        @pl.when(jnp.logical_not(is_self(n)))
        def _():
            kv_copy(n, c, r).start()

    loop(0, 16, kv_start)

    @pl.when(src_row == r)
    def _():
        kv_all[c] = kv_send[lax.rem(c, 2)]

    gather_start(wo_all, wo_ss, wo_rs)

    loop(12, 16, bias_group)

    def kv_take(h):
        @pl.when(jnp.logical_or(src_row != r, h != c))
        def _():
            kv_copy(0, h, r).wait_recv()

    loop(0, NC, kv_take)
    krow[...] = jnp.transpose(kv_all[:, 0:48, :].reshape(D, 128))
    vrow[...] = jnp.transpose(kv_all[:, 48:96, :].reshape(D, 128))
    gather_wait(da_all, da_ss, da_rs)
    darow[...] = jnp.transpose(da_all[...].reshape(D, 256)).reshape(NC, GT, D)
    gather_wait(q_all, q_ss, q_rs)
    qrow[...] = jnp.transpose(q_all[...].reshape(D, 256)).reshape(NC, GT, D)

    def st_copy(g, s):
        return pltpu.make_async_remote_copy(
            st_send.at[g], st_recv.at[s], st_ss.at[g], st_rs.at[s], device_id=(r, g), device_id_type=MESH
        )

    def score_group(k):
        g = lax.rem(c + k, NC)
        s = nt(krow[...], spread(qrow[g], mask)) * SCALE + bias[g]
        dp = nt(vrow[...], spread(darow[g], mask))
        m = jnp.max(s, axis=0, keepdims=True)
        e = jnp.exp(s - m)
        ebuf[g] = e
        dpbuf[g] = dp
        l = jnp.sum(e, axis=0, keepdims=True)
        t = jnp.sum(e * dp, axis=0, keepdims=True)
        z = jnp.zeros((2, 128), F32)
        st_send[g] = jnp.concatenate(
            [m[:, :128], m[:, 128:], l[:, :128], l[:, 128:], t[:, :128], t[:, 128:], z], axis=0
        )

        @pl.when(g != c)
        def _():
            st_copy(g, c).start()

    loop(1, NC + 1, score_group)
    st_recv[c] = st_send[c]

    def att_copy(g, s):
        return pltpu.make_async_remote_copy(
            att_send.at[g], att_recv.at[s], att_ss.at[g], att_rs.at[s], device_id=(r, g), device_id_type=MESH
        )

    pairs = head_tiles()

    def att_group(k):
        g = lax.rem(c + k, NC)
        et = jnp.transpose(ebuf[g].astype(BF))
        full = nn(et, vrow[...])
        cols = []
        for t in range(6):
            tot = None
            for h, t2 in pairs:
                if t2 == t:
                    sl = (slice(16 * h, 16 * h + 16), slice(128 * t, 128 * t + 128))
                    term = full[sl] * mask[sl].astype(F32)
                    tot = term if tot is None else tot + term
            cols.append(tot)
        att_send[g] = jnp.concatenate(cols, axis=1).astype(BF)

    loop(1, NC + 1, att_group)

    def st_take(k):
        s = lax.rem(c + NC - k, NC)
        st_copy(c, s).wait_recv()

    loop(1, NC, st_take)
    sr = st_recv[...]
    top = jnp.max(sr[:, 0:2, :], axis=0)
    fac = jnp.exp(sr[:, 0:2, :] - top[None])
    tot_l = jnp.sum(fac * sr[:, 2:4, :], axis=0)
    tot_t = jnp.sum(fac * sr[:, 4:6, :], axis=0)
    inv = 1.0 / tot_l
    fin_all[c] = jnp.concatenate([top, inv, tot_t * inv, jnp.zeros((2, 128), F32)], axis=0)
    gather_start(fin_all, fin_ss, fin_rs)

    def att_start(k):
        g = lax.rem(c + k, NC)
        att_copy(g, c).start()

    loop(1, NC, att_start)
    att_recv[c] = att_send[c]

    frow = fac * inv[None]
    fwide = jnp.concatenate([frow[:, 0, :], frow[:, 1, :]], axis=1)
    fbig = jnp.broadcast_to(fwide[:, None, :], (16, 16, 256))
    keep = lax.rem(lax.broadcasted_iota(jnp.int32, (16, 16, 256), 2), 16) == lax.broadcasted_iota(
        jnp.int32, (16, 16, 256), 1
    )
    fbig = jnp.where(keep, fbig, 0.0).reshape(256, 256)
    f_hi = fbig.astype(BF)
    f_lo = (fbig - f_hi.astype(F32)).astype(BF)
    f_all = (nn(f_hi, mask[...]) + nn(f_lo, mask[...])).reshape(16, 16, D)

    gather_wait(fin_all, fin_ss, fin_rs)

    def d_copy(g):
        return pltpu.make_async_copy(dbuf.at[g], d_out.at[g], d_sem.at[g])

    def d_group(g):
        fin = fin_all[g]
        own = st_send[g]
        scale = jnp.exp(own[0:2] - fin[0:2]) * fin[2:4]
        scale = jnp.concatenate([scale[0:1], scale[1:2]], axis=1)
        inner = jnp.concatenate([fin[4:5], fin[5:6]], axis=1)
        d = ((ebuf[g] * scale) * (dpbuf[g] - inner)).astype(BF)
        dbuf[g] = d
        dt[g] = jnp.transpose(d)
        d_copy(g).start()

    loop(0, 16, d_group)

    lhs_w = jnp.concatenate([dt[g] for g in range(NC)], axis=1)
    ii = lax.broadcasted_iota(jnp.int32, (16, 16, 128), 1)
    wcol[c] = jnp.zeros((16, 128), F32)

    def weight_step(n):
        rhs = jnp.concatenate(
            [jnp.concatenate([pairv[g * GT + 2 * n], pairv[g * GT + 2 * n + 1]], axis=1) for g in range(NC)], axis=0
        )
        full = nn(lhs_w, rhs).reshape(16, 16, 256)
        one = jnp.where(ii == 2 * n, full[:, :, 0:128], 0.0) + jnp.where(ii == 2 * n + 1, full[:, :, 128:256], 0.0)
        wcol[c] = wcol[c] + jnp.sum(one, axis=1)

    loop(0, 8, weight_step)
    gather_start(wcol, wc_ss, wc_rs)

    def att_take(k):
        s = lax.rem(c + NC - k, NC)
        att_copy(c, s).wait_recv()

    loop(1, NC, att_take)
    att = jnp.sum(att_recv[...].astype(F32) * f_all, axis=0).astype(BF)
    gather_wait(wo_all, wo_ss, wo_rs)
    proj = nn(att, wo_all[...].reshape(D, D))
    upd_out[...] = (single_v[...].astype(F32) + proj).astype(BF)

    gather_wait(wcol, wc_ss, wc_rs)
    wrow[r] = jnp.sum(wcol[...], axis=0)

    def wr_copy(peer, slot):
        return pltpu.make_async_remote_copy(
            wrow.at[slot], wrow.at[slot], wr_ss.at[peer], wr_rs.at[slot], device_id=(peer, c), device_id_type=MESH
        )

    loop(1, NR, lambda k: wr_copy(lax.rem(r + k, NR), r).start())

    def pool_sent(o):
        @pl.when(sends_to(c, o))
        def _():
            pool_copy(o, c).wait_send()

    loop(0, NC, pool_sent)
    gather_sent(cot_all, cot_ss, cot_rs)
    gather_sent(norm_all, norm_ss, norm_rs)
    gather_sent(da_all, da_ss, da_rs)
    gather_sent(q_all, q_ss, q_rs)
    gather_sent(wo_all, wo_ss, wo_rs)
    gather_sent(fin_all, fin_ss, fin_rs)
    gather_sent(wcol, wc_ss, wc_rs)

    def kv_sent(n):
        @pl.when(jnp.logical_not(is_self(n)))
        def _():
            kv_copy(n, c, r).wait_send()

    loop(0, 16, kv_sent)

    def st_sent(k):
        g = lax.rem(c + k, NC)
        st_copy(g, c).wait_send()
        att_copy(g, c).wait_send()

    loop(1, NC, st_sent)
    loop(0, 16, lambda g: d_copy(g).wait())

    def wr_take(k):
        p = lax.rem(r + NR - k, NR)
        wr_copy(p, p).wait_recv()

    loop(1, NR, wr_take)
    loop(1, NR, lambda k: wr_copy(lax.rem(r + k, NR), r).wait_send())
    wg_out[...] = jnp.sum(wrow[...], axis=0)


def grad_kernel(d, w_pair, upd, wg, upd_out, grad, wg_out, w2, out, sem):
    upd_out[...] = upd[...]
    wide = jnp.concatenate([wg[...], jnp.zeros((112, 128), F32)], axis=0)
    wg_out[...] = jnp.transpose(wide)[:, 0:16]
    rowi = lax.broadcasted_iota(jnp.int32, (256, 16), 0)
    lani = lax.broadcasted_iota(jnp.int32, (256, 16), 1)
    rep = jnp.where(rowi // 16 == lani, 1.0, 0.0).astype(BF)
    wrep = nt(rep, w_pair[...])
    rowm = lax.rem(lax.broadcasted_iota(jnp.int32, (256, 128), 0), 16)
    for i in range(GT):
        w2[:, 128 * i : 128 * i + 128] = jnp.where(rowm == i, wrep, 0.0).astype(BF)

    def copy(g):
        return pltpu.make_async_copy(out.at[pl.ds(g * GT, GT)], grad.at[pl.ds(g * GT, GT)], sem.at[g])

    def step(g, carry):
        full = nn(d[g], w2[...]).astype(BF)
        for i in range(GT):
            out[g * GT + i] = full[:, 128 * i : 128 * i + 128]
        copy(g).start()
        return carry

    lax.fori_loop(0, 16, step, 0)

    def done(g, carry):
        copy(g).wait()
        return carry

    lax.fori_loop(0, 16, done, 0)


def on_device(atom_feats, atom_counts, w_atom, single_in, w_qkv, w_out, pair, w_pair, cotangent):
    vm = pl.BlockSpec(memory_space=pltpu.VMEM)
    hbm = pl.BlockSpec(memory_space=pl.ANY)
    V = pltpu.VMEM
    dma = pltpu.SemaphoreType.DMA
    sems16 = dma((16,))
    d_bias, upd, wg = pl.pallas_call(
        main_kernel,
        name="attend",
        out_shape=(
            jax.ShapeDtypeStruct((16, 128, 256), BF),
            jax.ShapeDtypeStruct((16, D), BF),
            jax.ShapeDtypeStruct((16, 128), F32),
        ),
        in_specs=[vm, vm, vm, vm, vm, vm, hbm, vm, vm],
        out_specs=(hbm, vm, vm),
        scratch_shapes=[
            V((256, 128, 128), BF),
            V((16, 16, D), BF),
            V((16, 16, D), BF),
            V((16, D), F32),
            V((16, 16, D), BF),
            V((16, 16, D), BF),
            V((16, 48, D), BF),
            V((2, 96, 128), BF),
            V((16, 96, 128), BF),
            V((16, 48, 256), BF),
            V((16, 48, 256), BF),
            V((2048, 256), BF),
            V((144, D), BF),
            V((256, D), BF),
            V((16, 128, 256), F32),
            V((16, 128, 256), F32),
            V((16, 128, 256), F32),
            V((16, 8, 128), F32),
            V((16, 8, 128), F32),
            V((16, 8, 128), F32),
            V((16, 16, D), BF),
            V((16, 16, D), BF),
            V((16, 128, 256), BF),
            V((16, 256, 128), BF),
            V((16, 16, 128), F32),
            V((8, 16, 128), F32),
            V((128, D), BF),
            V((128, D), BF),
            V((16, 16, D), BF),
            V((16, 16, D), BF),
            V((16, D), BF),
            sems16,
            sems16,
        ]
        + [sems16] * 22
        + [dma((8,))] * 2,
        compiler_params=pltpu.CompilerParams(collective_id=0, has_side_effects=True, vmem_limit_bytes=56 << 20),
    )(
        atom_feats,
        atom_counts.reshape(16, 128),
        w_atom,
        single_in,
        w_qkv,
        w_out,
        pair,
        w_pair,
        cotangent,
    )
    updated, grad_pair, grad_w = pl.pallas_call(
        grad_kernel,
        name="grad_pair",
        out_shape=(
            jax.ShapeDtypeStruct((16, D), BF),
            jax.ShapeDtypeStruct((256, 128, 128), BF),
            jax.ShapeDtypeStruct((128, 16), F32),
        ),
        in_specs=[vm, vm, vm, vm],
        out_specs=(vm, hbm, vm),
        scratch_shapes=[V((256, 2048), BF), V((256, 128, 128), BF), sems16],
        compiler_params=pltpu.CompilerParams(vmem_limit_bytes=48 << 20),
    )(d_bias, w_pair, upd, wg)
    return updated, grad_pair, grad_w


def solution(mesh):
    placed = (
        P(("row", "col"), None),
        P(),
        P(),
        P(("row", "col"), None),
        P(None, None, "col"),
        P("col", None),
        P("row", "col", None),
        P(),
        P(("row", "col"), None),
    )
    return jax.shard_map(
        on_device,
        mesh=mesh,
        in_specs=placed,
        out_specs=(P(("row", "col"), None), P("row", "col", None), P()),
        check_vma=False,
    )
```

time: 353 us -> 107 us (0.30)
  blocking collectives: 170 us -> 0 us
  Pallas kernels: 0 us -> 99.5 us
  waiting for transfers between devices: 85.7 us -> 0 us
  matrix products: 25.4 us -> 0 us
  starting transfers between devices: 25.3 us -> 0 us
  other arithmetic: 19.3 us -> 0 us
  between operations: 14.2 us -> 0.67 us
  local copies, waits for them, and re-layouts: 12.2 us -> 6.72 us
    all_gather x4 -> x0, blocking collectives: 104 us -> none  [the longest x1 31.7 us: on_device(): cot_rows = lax.all_gather(cotangent, 'col', axis=0, tiled=True)]
    pallas_call x0 -> x2, Pallas kernels: none -> 99.5 us  [the longest x1 92.6 us: on_device(): pl.pallas_call(main_kernel, name='attend', out_shape=(jax.ShapeDtypeStruc...]
    reduce_scatter x2 -> x0, waiting for transfers between devices: 85.7 us -> none  [the longest x1 66 us: on_device(): lax.psum_scatter(jnp.dot(attended, w_out, preferred_element_type=jnp.floa...]
    psum x1 -> x0, blocking collectives: 66.3 us -> none  [on_device(): grad_pair_weight = lax.psum(weight_part, ('row', 'col'))]
    dot_general x9 -> x0, matrix products: 25.4 us -> none  [the longest x1 5.66 us: on_device(): jnp.einsum('ijc,ch->hij', pair, w_pair, preferred_element_type=jnp.float32)]
    all_to_all x2 -> x0, starting transfers between devices: 25 us -> none  [the longest x1 16.5 us: on_device(): lax.all_to_all(d_bias, 'col', split_axis=2, concat_axis=0, tiled=True)]
    unnamed x1 -> x0, other arithmetic: 11.6 us -> none
    convert_element_type x3 -> x0, local copies, waits for them, and re-layouts: 7.54 us -> none  [the longest x1 3.75 us: on_device(): d_bias = (probs * (d_probs - inner)).astype(jnp.bfloat16)]
  transfers between devices with their start and end apart: 4 -> 0, of which waited for: 2 -> 0; matrix products, arithmetic and copies ran while one was open for 4% -> 0% of each run, Pallas kernels for 0% -> 0%
where the time goes in v1:
time: 107 us
  Pallas kernels  99.5 us (93%)
  local copies, waits for them, and re-layouts  6.72 us (6%)
    pallas_call x1, Pallas kernels, on_device(): pl.pallas_call(main_kernel, name='attend', out_shape=(jax.ShapeDtypeStruc...  92.6 us
    pallas_call x1, Pallas kernels, on_device(): pl.pallas_call(grad_kernel, name='grad_pair', out_shape=(jax.ShapeDtypeSt...  6.96 us
    unnamed x10, local copies, waits for them, and re-layouts  6.05 us

profile of v1, /device:TPU:1, one launch (start us, length us, event | category | flops | bytes accessed | tf_op | source)
XLA Modules:
  0.0 106.9 jit_solution(18346595282168947743)
XLA Ops:
  0.6 1.4 %copy.13.w_pair = bf16[128,16]{1,0:T(8,128)(2,1)} copy(bf16[128,16]{0,1:T(8,128)(2,1)} %param.16) | data formatting | bytes 8192 | tf_op args[7]
  2.0 0.0 copy-start.1
  2.0 2.0 %copy.12.w_qkv = bf16[3,768,48]{2,1,0:T(8,128)(2,1)} copy(bf16[3,768,48]{1,2,0:T(8,128)(2,1)} %param.13) | data formatting | bytes 442368 | tf_op args[4]
  4.0 92.6 %attend.1 = (bf16[16,128,256]{2,1,0:T(8,128)(2,1)}, bf16[16,768]{1,0:T(8,128)(2,1)}, f32[16,128]{1,0:T(8,128)}) custom-call(bf16[160,128]{1,0:T(8,128)(2,1)} %feats.1, s32[16,128]{1,0:T(8,128)} %bitcast.1, bf16[128,768]{1,0:T(8,128)(2,1)} %w_atom.1, bf16[16,768]{1,0:T(8,128)(2,1)} %single_in.1, bf16[3,768,48]{2,1,0:T(8,128)(2,1)} %copy.12.w_qkv, ...), custom_call_target="tpu_custom_call" | custom-call | tf_op jit(solution)/shard_map/attend/pallas_call | solution.py:469
  96.6 0.0 copy-done.1
  96.6 0.0 copy-start
  96.6 1.2 %copy-done = bf16[16,128,256]{2,1,0:T(8,128)(2,1)S(1)} copy-done((bf16[16,128,256]{2,1,0:T(8,128)(2,1)S(1)}, bf16[16,128,256]{2,1,0:T(8,128)(2,1)}, u32[]{:S(2)}) %copy-start) | copy-done | bytes 1048600
  97.8 0.0 copy-start.2
  97.8 0.7 copy-done.2
  98.6 0.0 copy-start.3
  98.6 0.7 copy-done.3
  99.3 7.0 %grad_pair.1 = (bf16[16,768]{1,0:T(8,128)(2,1)}, bf16[256,128,128]{2,1,0:T(8,128)(2,1)}, f32[128,16]{1,0:T(8,128)S(1)}) custom-call(bf16[16,128,256]{2,1,0:T(8,128)(2,1)S(1)} %copy-done, bf16[128,16]{1,0:T(8,128)(2,1)S(1)} %copy-done.1, bf16[16,768]{1,0:T(8,128)(2,1)S(1)} %copy-done.2, f32[16,128]{1,0:T(8,128)S(1)} %copy-done.3), custom_call_target="tpu_custom_call" | custom-call | tf_op jit(solution)/shard_map/grad_pair/pallas_call | solution.py:528
  106.2 0.7 copy.15
Async XLA Ops:
  2.0 94.6 %copy-start.1 = (bf16[128,16]{1,0:T(8,128)(2,1)S(1)}, bf16[128,16]{1,0:T(8,128)(2,1)}, u32[]{:S(2)}) copy-start(bf16[128,16]{1,0:T(8,128)(2,1)} %copy.13.w_pair) | copy-start | bytes 12292
  96.6 1.2 %copy-start = (bf16[16,128,256]{2,1,0:T(8,128)(2,1)S(1)}, bf16[16,128,256]{2,1,0:T(8,128)(2,1)}, u32[]{:S(2)}) copy-start(bf16[16,128,256]{2,1,0:T(8,128)(2,1)} %get-tuple-element.6.d) | copy-start | bytes 3145732
  97.8 0.7 copy-start.2
  98.6 0.7 copy-start.3

commit v2 on v0

v2 whole, which is shorter than its diff:
```python
import jax
import jax.numpy as jnp
from jax import lax
from jax.experimental import pallas as pl
from jax.experimental.pallas import tpu as pltpu
from jax.sharding import PartitionSpec as P

MESH = pl.DeviceIdType.MESH
BF = jnp.bfloat16
F32 = jnp.float32
NC = 16
NR = 8
HD = 48
HP = 64
D = 768
DP = NC * HP
GT = 16
SCALE = 1.0 / (48.0**0.5)


def nt(a, b):
    return lax.dot_general(a, b, (((1,), (1,)), ((), ())), preferred_element_type=F32)


def nn(a, b):
    return jnp.dot(a, b, preferred_element_type=F32)


def loop(lo, hi, body):
    def step(k, carry):
        body(k)
        return carry

    lax.fori_loop(lo, hi, step, 0)


def iota(shape, dim):
    return lax.broadcasted_iota(jnp.int32, shape, dim)


def to_row(col):
    eye = iota((128, 128), 0) == iota((128, 128), 1)
    return [
        jnp.sum(jnp.where(eye, col[128 * n : 128 * n + 128], 0.0), axis=0, keepdims=True)
        for n in range(2)
    ]


def lane_sum(x):
    return jnp.broadcast_to(jnp.sum(x, axis=1, keepdims=True), x.shape)


def to_col(rows):
    eye = iota((128, 128), 0) == iota((128, 128), 1)
    return lane_sum(
        jnp.concatenate([jnp.where(eye, jnp.broadcast_to(rows[n : n + 1], (128, 128)), 0.0) for n in range(2)], axis=0)
    )


def main_kernel(
    feats, counts, w_atom, single_in, w_qkv, w_out, pair, w_pair, cot,
    d_out, upd_out, wg_out,
    pairv, feats_v, counts_v, w_atom_v, single_in_v, wt, wp_v,
    part, pool_recv, acc, norm_all, cot_all, wo_all, kv_row, kv_all, q_all, da_all,
    wbd, maskp, bias, sbuf, dpbuf, eb, st_send, st_recv, fin_all, att_send, att_recv,
    dbuf, dt, wcol, wrow, vrow, qrow, darow, single_v, upd_v, wg_v,
    in_sem, pair_sem, d_sem, out_sem,
    pool_ss, pool_rs, norm_ss, norm_rs, cot_ss, cot_rs, wo_ss, wo_rs, kv_ss, kv_rs, q_ss, q_rs,
    da_ss, da_rs, st_ss, st_rs, fin_ss, fin_rs, att_ss, att_rs, wc_ss, wc_rs, kvr_ss, kvr_rs, wr_ss, wr_rs,
):
    r = lax.axis_index("row")
    c = lax.axis_index("col")
    chip = c // 2
    core = lax.rem(c, 2)
    mate = 2 * chip + 1 - core

    ins = [
        pltpu.make_async_copy(a, b, in_sem.at[n])
        for n, (a, b) in enumerate(
            [
                (feats, feats_v.at[pl.ds(0, 160)]),
                (counts, counts_v),
                (w_atom, w_atom_v),
                (w_pair, wp_v),
                (cot, cot_all.at[c]),
                (single_in, single_in_v),
                (w_out, wo_all.at[c, pl.ds(0, HD)]),
                (w_qkv, wt),
            ]
        )
    ]
    for cp in ins:
        cp.start()

    def pair_copy(g):
        return pltpu.make_async_copy(pair.at[pl.ds(g * GT, GT)], pairv.at[pl.ds(g * GT, GT)], pair_sem.at[g])

    loop(0, 16, lambda g: pair_copy(g).start())

    bar = pltpu.get_barrier_semaphore()

    def greet_col(k):
        pl.semaphore_signal(bar, inc=1, device_id=(r, lax.rem(c + k, NC)), device_id_type=MESH)

    def greet_row(k):
        pl.semaphore_signal(bar, inc=1, device_id=(lax.rem(r + k, NR), c), device_id_type=MESH)

    loop(1, NC, greet_col)
    loop(1, NR, greet_row)

    feats_v[160:256, :] = jnp.zeros((96, 128), BF)
    ins[1].wait()
    crow = jnp.concatenate([counts_v[pl.ds(2 * r, 1), :], counts_v[pl.ds(2 * r + 1, 1), :]], axis=1).astype(F32)
    tok = iota((256, 256), 0)
    lan = iota((256, 256), 1)
    cbig = jnp.broadcast_to(crow, (256, 256))
    ends = jnp.sum(jnp.where(lan <= tok, cbig, 0.0), axis=1, keepdims=True)
    cnt = jnp.sum(jnp.where(lan == tok, cbig, 0.0), axis=1, keepdims=True)
    atom = (lan + 160 * c).astype(F32)
    inside = jnp.logical_and(jnp.logical_and(atom < ends, atom >= ends - cnt), lan < 160)
    onehot = jnp.where(inside, 1.0, 0.0).astype(BF)
    ins[0].wait()
    ins[2].wait()
    hidden = jnp.maximum(nn(feats_v[...], w_atom_v[...]), 0.0).astype(BF)
    part[...] = (nn(onehot, hidden) / cnt).astype(BF).reshape(NC, GT, D)

    ins[3].wait()
    rep = jnp.where(iota((256, 16), 0) // 16 == iota((256, 16), 1), 1.0, 0.0).astype(BF)
    wrep = lax.dot_general(wp_v[...], rep, (((0,), (1,)), ((), ())), preferred_element_type=F32)
    lanw = lax.rem(iota((128, 256), 1), 16)
    for i in range(GT):
        wbd[128 * i : 128 * i + 128, :] = jnp.where(lanw == i, wrep, 0.0).astype(BF)
    maskp[...] = jnp.where(iota((256, DP), 1) // HP == iota((256, DP), 0) // GT, 1.0, 0.0).astype(BF)
    pad = jnp.zeros((NC, HP - HD, 256), BF)
    q_all[:, HD:HP, :] = pad
    da_all[:, HD:HP, :] = pad
    kv_all[:, 0, HD:HP, :] = pad[:, :, 0:128]
    kv_all[:, 1, HD:HP, :] = pad[:, :, 0:128]
    wo_all[:, HD:HP, :] = jnp.zeros((NC, HP - HD, D), BF)
    for n in range(4, 8):
        ins[n].wait()

    pl.semaphore_wait(bar, 22)

    def lo(s):
        return (160 * s) // 384

    def hi(s):
        return jnp.where(s == 15, 15, jnp.minimum(6, (160 * s + 159) // 304))

    def pool_copy(o, s):
        return pltpu.make_async_remote_copy(
            part.at[o], pool_recv.at[s], pool_ss.at[o], pool_rs.at[s], device_id=(r, o), device_id_type=MESH
        )

    def sends_to(s, o):
        return jnp.logical_and(jnp.logical_and(o >= lo(s), o <= hi(s)), o != s)

    def pool_start(o):
        @pl.when(sends_to(c, o))
        def _():
            pool_copy(o, c).start()

    loop(0, NC, pool_start)

    def piece(buf, slot, rows):
        return buf.at[slot] if rows is None else buf.at[slot, pl.ds(0, rows)]

    def gather_copy(buf, rows, ss, rs, peer, slot, n):
        return pltpu.make_async_remote_copy(
            piece(buf, slot, rows), piece(buf, slot, rows), ss.at[n], rs.at[slot], device_id=(r, peer), device_id_type=MESH
        )

    def near(k):
        return 2 * lax.rem(chip + k, 8) + core

    def gather_start(buf, rows, ss, rs):
        gather_copy(buf, rows, ss, rs, mate, c, 0).start()
        loop(1, 8, lambda k: gather_copy(buf, rows, ss, rs, near(k), c, k).start())

    def gather_relay(buf, rows, ss, rs):
        def body(k):
            slot = near(8 - k)
            gather_copy(buf, rows, ss, rs, slot, slot, k).wait_recv()
            gather_copy(buf, rows, ss, rs, mate, slot, 8 + k).start()

        loop(1, 8, body)

    def gather_end(buf, rows, ss, rs):
        def body(k):
            slot = 2 * lax.rem(chip + 8 - k, 8) + 1 - core
            gather_copy(buf, rows, ss, rs, mate, slot, 0).wait_recv()

        loop(0, 8, body)

    def gather_sent(buf, rows, ss, rs):
        def body(k):
            gather_copy(buf, rows, ss, rs, near(k), c, k).wait_send()
            gather_copy(buf, rows, ss, rs, mate, c, 8 + k).wait_send()

        gather_copy(buf, rows, ss, rs, mate, c, 0).wait_send()
        loop(1, 8, body)

    g_cot = (cot_all, None, cot_ss, cot_rs)
    g_norm = (norm_all, None, norm_ss, norm_rs)
    g_da = (da_all, HD, da_ss, da_rs)
    g_q = (q_all, HD, q_ss, q_rs)
    g_wo = (wo_all, HD, wo_ss, wo_rs)

    gather_start(*g_cot)

    def bias_group(g):
        pair_copy(g).wait()
        lhs = jnp.concatenate([pairv[g * GT + i] for i in range(GT)], axis=1)
        bias[g] = jnp.transpose(nn(lhs, wbd[...]).astype(BF))

    loop(0, 3, bias_group)

    acc[...] = single_in_v[...].astype(F32) + part[c].astype(F32)

    def pool_take(s):
        @pl.when(sends_to(s, c))
        def _():
            pool_copy(c, s).wait_recv()
            acc[...] += pool_recv[s].astype(F32)

    loop(0, NC, pool_take)
    single = acc[...].astype(BF)
    single_v[...] = single
    v32 = single.astype(F32)
    center = jnp.mean(v32, axis=1, keepdims=True)
    diff = v32 - center
    var = jnp.mean(diff * diff, axis=1, keepdims=True)
    norm_all[c] = (diff / jnp.sqrt(var + 1e-05)).astype(BF)
    gather_start(*g_norm)

    gather_relay(*g_cot)
    loop(3, 6, bias_group)
    gather_end(*g_cot)
    da_all[c, 0:HD] = nt(wo_all[c, 0:HD], cot_all[...].reshape(256, D)).astype(BF)
    gather_start(*g_da)

    loop(6, 10, bias_group)

    gather_relay(*g_norm)
    gather_end(*g_norm)
    qkv = nt(wt[...].reshape(3 * HD, D), norm_all[...].reshape(256, D)).astype(BF)
    q_all[c, 0:HD] = qkv[0:HD]
    for half in range(2):
        for n in range(2):
            kv_row[r, half, n] = qkv[HD * (n + 1) : HD * (n + 2), 128 * half : 128 * half + 128]

    def kvr_copy(peer, slot):
        return pltpu.make_async_remote_copy(
            kv_row.at[slot], kv_row.at[slot], kvr_ss.at[peer], kvr_rs.at[slot], device_id=(peer, c), device_id_type=MESH
        )

    loop(1, NR, lambda k: kvr_copy(lax.rem(r + k, NR), r).start())
    gather_start(*g_q)

    def kv_copy(b, half, s):
        return pltpu.make_async_remote_copy(
            kv_row.at[b, half],
            kv_all.at[s, :, pl.ds(0, HD)],
            kv_ss.at[2 * b + half],
            kv_rs.at[s],
            device_id=(r, 2 * b + half),
            device_id_type=MESH,
        )

    def kv_forward(b):
        for half in range(2):
            @pl.when(2 * b + half != c)
            def _(half=half):
                kv_copy(b, half, c).start()

            @pl.when(2 * b + half == c)
            def _(half=half):
                kv_all[c, :, 0:HD, :] = kv_row[b, half]

    kv_forward(r)
    gather_relay(*g_da)
    loop(10, 12, bias_group)

    def kvr_take(k):
        b = lax.rem(r + NR - k, NR)
        kvr_copy(b, b).wait_recv()
        kv_forward(b)

    loop(1, NR, kvr_take)
    gather_relay(*g_q)
    loop(12, 16, bias_group)

    gather_end(*g_da)
    dat = jnp.transpose(da_all[...].reshape(DP, 256))
    for m in range(4):
        darow[m] = dat[:, 256 * m : 256 * m + 256].reshape(NC, GT, 256)
    gather_end(*g_q)
    qt = jnp.transpose(q_all[...].reshape(DP, 256))
    for m in range(4):
        qrow[m] = qt[:, 256 * m : 256 * m + 256].reshape(NC, GT, 256)

    def kv_take(h):
        @pl.when(h != c)
        def _():
            kv_copy(0, 0, h).wait_recv()

    loop(0, NC, kv_take)

    lan128 = iota((16, 128), 1)
    first = jnp.where(lan128 < HP, 1.0, 0.0).astype(BF)
    second = jnp.where(lan128 >= HP, 1.0, 0.0).astype(BF)
    none = jnp.zeros((16, 128), BF)

    def spread(rows_ref, m):
        out = []
        for g in range(NC):
            a, b = rows_ref[m, g, :, 0:128], rows_ref[m, g, :, 128:256]
            out += [
                jnp.concatenate([a * first, none], axis=1),
                jnp.concatenate([a * second, none], axis=1),
                jnp.concatenate([none, b * first], axis=1),
                jnp.concatenate([none, b * second], axis=1),
            ]
        return jnp.concatenate(out, axis=0)

    def quad(m):
        kt = kv_all[4 * m : 4 * m + 4, 0].reshape(4 * HP, 128)
        vt = kv_all[4 * m : 4 * m + 4, 1].reshape(4 * HP, 128)
        sbuf[m] = nn(spread(qrow, m), kt).reshape(NC, 64, 128)
        dpbuf[m] = nn(spread(darow, m), vt).reshape(NC, 64, 128)
        vrow[2 * m] = jnp.transpose(vt[0:128])
        vrow[2 * m + 1] = jnp.transpose(vt[128:256])

    for m in range(4):
        quad(m)
    gather_start(*g_wo)

    def st_copy(g, s):
        return pltpu.make_async_remote_copy(
            st_send.at[g], st_recv.at[s], st_ss.at[g], st_rs.at[s], device_id=(r, g), device_id_type=MESH
        )

    U = 4

    def soft_step(q):
        gs = [U * q + u for u in range(U)]
        s = jnp.concatenate([sbuf[m, g] for g in gs for m in range(4)], axis=0)
        b = jnp.concatenate([bias[g] for g in gs], axis=0)
        dp = jnp.concatenate([dpbuf[m, g] for g in gs for m in range(4)], axis=0)
        s = s * SCALE + b.astype(F32)
        top = jnp.max(s, axis=1, keepdims=True)
        e = jnp.exp(s - top)
        l = lane_sum(e)
        t = lane_sum(e * dp)
        e16 = e.astype(BF)
        top = jnp.broadcast_to(top, e.shape)
        stats = []
        for u in range(U):
            part_of = slice(256 * u, 256 * u + 256)
            rows = to_row(top[part_of]) + to_row(l[part_of]) + to_row(t[part_of]) + [jnp.zeros((2, 128), F32)]
            stats.append(jnp.concatenate(rows, axis=0))
        for u, g in enumerate(gs):
            for m in range(4):
                k = 256 * u + 64 * m
                sbuf[m, g] = e[k : k + 64]
                eb[m, g] = e16[k : k + 64]
            st_send[g] = stats[u]
        for g in gs:
            @pl.when(g != c)
            def _(g=g):
                st_copy(g, c).start()

    loop(0, NC // U, soft_step)
    st_recv[c] = st_send[c]

    def att_copy(g, s):
        return pltpu.make_async_remote_copy(
            att_send.at[g], att_recv.at[s], att_ss.at[g], att_rs.at[s], device_id=(r, g), device_id_type=MESH
        )

    keep = iota((16, 16, 128), 2) < HP
    for p in range(8):
        rows = eb[p // 2, :, 32 * (p % 2) : 32 * (p % 2) + 32, :].reshape(512, 128)
        full = nn(rows, vrow[p]).reshape(NC, 2, GT, 128)
        att_send[:, :, 128 * p : 128 * p + 128] = jnp.where(keep, full[:, 0], full[:, 1]).astype(BF)

    loop(1, NC, lambda k: st_copy(c, lax.rem(c + NC - k, NC)).wait_recv())
    sr = st_recv[...]
    best = jnp.max(sr[:, 0:2, :], axis=0)
    fac = jnp.exp(sr[:, 0:2, :] - best[None])
    tot_l = jnp.sum(fac * sr[:, 2:4, :], axis=0)
    tot_t = jnp.sum(fac * sr[:, 4:6, :], axis=0)
    inv = 1.0 / tot_l
    fin_all[c] = jnp.concatenate([best, inv, tot_t * inv, jnp.zeros((2, 128), F32)], axis=0)

    def fin_copy(peer, slot):
        return pltpu.make_async_remote_copy(
            fin_all.at[slot], fin_all.at[slot], fin_ss.at[peer], fin_rs.at[slot], device_id=(r, peer), device_id_type=MESH
        )

    loop(1, NC, lambda k: fin_copy(lax.rem(c + k, NC), c).start())
    loop(1, NC, lambda k: att_copy(lax.rem(c + k, NC), c).start())
    att_recv[c] = att_send[c]

    frow = fac * inv[None]
    fwide = jnp.concatenate([frow[:, 0, :], frow[:, 1, :]], axis=1)
    fbig = jnp.broadcast_to(fwide[:, None, :], (16, 16, 256))
    diag = lax.rem(iota((16, 16, 256), 2), 16) == iota((16, 16, 256), 1)
    fbig = jnp.where(diag, fbig, 0.0).reshape(256, 256)
    f_hi = fbig.astype(BF)
    f_lo = (fbig - f_hi.astype(F32)).astype(BF)
    f_all = (nn(f_hi, maskp[...]) + nn(f_lo, maskp[...])).reshape(16, 16, DP)
    gather_relay(*g_wo)

    def d_copy(g):
        return pltpu.make_async_copy(dt.at[g], d_out.at[g], d_sem.at[g])

    loop(1, NC, lambda k: fin_copy(c, lax.rem(c + NC - k, NC)).wait_recv())

    W = 8

    def d_step(q):
        gs = [W * q + u for u in range(W)]
        scale, inner = [], []
        for g in gs:
            fin, own = fin_all[g], st_send[g]
            scale.append(to_col(jnp.exp(own[0:2] - fin[0:2]) * fin[2:4]))
            inner.append(to_col(fin[4:6]))
        e = jnp.concatenate([sbuf[m, g] for g in gs for m in range(4)], axis=0)
        dp = jnp.concatenate([dpbuf[m, g] for g in gs for m in range(4)], axis=0)
        d = (e * jnp.concatenate(scale, axis=0)) * (dp - jnp.concatenate(inner, axis=0))
        dbuf[pl.ds(W * q, W)] = d.reshape(W, 256, 128)

    loop(0, NC // W, d_step)

    def weight_step(q):
        lhs = [dbuf[4 * q + n, pl.ds(i, NC, stride=GT), :] for n in range(4) for i in range(GT)]
        rhs = pairv[pl.ds(4 * GT * q, 4 * GT)].reshape(4 * GT * 128, 128)
        return nn(jnp.concatenate(lhs, axis=1).astype(BF), rhs)

    wcol[c] = lax.fori_loop(0, 4, lambda q, tot: tot + weight_step(q), jnp.zeros((16, 128), F32))

    def wc_copy(peer, slot):
        return pltpu.make_async_remote_copy(
            wcol.at[slot], wcol.at[slot], wc_ss.at[peer], wc_rs.at[slot], device_id=(r, peer), device_id_type=MESH
        )

    loop(1, NC, lambda k: wc_copy(lax.rem(c + k, NC), c).start())

    def d_turn(g):
        dt[g] = jnp.transpose(dbuf[g].astype(BF))
        d_copy(g).start()

    loop(0, 16, d_turn)

    loop(1, NC, lambda k: att_copy(c, lax.rem(c + NC - k, NC)).wait_recv())
    att = jnp.sum(att_recv[...].astype(F32) * f_all, axis=0).astype(BF)
    gather_end(*g_wo)
    proj = nn(att, wo_all[...].reshape(DP, D))
    upd_v[...] = (single_v[...].astype(F32) + proj).astype(BF)
    upd_copy = pltpu.make_async_copy(upd_v, upd_out, out_sem.at[0])
    upd_copy.start()

    loop(1, NC, lambda k: wc_copy(c, lax.rem(c + NC - k, NC)).wait_recv())
    wrow[r] = jnp.sum(wcol[...], axis=0)

    def wr_copy(peer, slot):
        return pltpu.make_async_remote_copy(
            wrow.at[slot], wrow.at[slot], wr_ss.at[peer], wr_rs.at[slot], device_id=(peer, c), device_id_type=MESH
        )

    loop(1, NR, lambda k: wr_copy(lax.rem(r + k, NR), r).start())

    def pool_sent(o):
        @pl.when(sends_to(c, o))
        def _():
            pool_copy(o, c).wait_send()

    loop(0, NC, pool_sent)
    for g in (g_cot, g_norm, g_da, g_q, g_wo):
        gather_sent(*g)
    loop(1, NR, lambda k: kvr_copy(lax.rem(r + k, NR), r).wait_send())

    def kv_sent(b):
        for half in range(2):
            @pl.when(2 * b + half != c)
            def _(half=half):
                kv_copy(b, half, c).wait_send()

    loop(0, NR, kv_sent)

    def col_sent(k):
        p = lax.rem(c + k, NC)
        st_copy(p, c).wait_send()
        att_copy(p, c).wait_send()
        fin_copy(p, c).wait_send()
        wc_copy(p, c).wait_send()

    loop(1, NC, col_sent)
    loop(0, 16, lambda g: d_copy(g).wait())
    upd_copy.wait()
    loop(1, NR, lambda k: wr_copy(r, lax.rem(r + NR - k, NR)).wait_recv())
    loop(1, NR, lambda k: wr_copy(lax.rem(r + k, NR), r).wait_send())
    wg_v[...] = jnp.sum(wrow[...], axis=0)
    wg_copy = pltpu.make_async_copy(wg_v, wg_out, out_sem.at[1])
    wg_copy.start()
    wg_copy.wait()


def grad_kernel(d, w_pair, upd, wg, upd_out, grad, wg_out, dv, wp_v, w2, out, in_sem, d_sem, sem):
    small = [
        pltpu.make_async_copy(w_pair, wp_v, in_sem.at[0]),
        pltpu.make_async_copy(upd, upd_out, in_sem.at[1]),
        pltpu.make_async_copy(wg, wg_out, in_sem.at[2]),
    ]
    for cp in small:
        cp.start()

    def d_copy(g):
        return pltpu.make_async_copy(d.at[g], dv.at[g], d_sem.at[g])

    loop(0, 16, lambda g: d_copy(g).start())
    rep = jnp.where(iota((256, 16), 0) // 16 == iota((256, 16), 1), 1.0, 0.0).astype(BF)
    small[0].wait()
    wrep = nn(rep, wp_v[...])
    rowm = lax.rem(iota((256, 128), 0), 16)
    for i in range(GT):
        w2[:, 128 * i : 128 * i + 128] = jnp.where(rowm == i, wrep, 0.0).astype(BF)

    def copy(g):
        return pltpu.make_async_copy(out.at[pl.ds(g * GT, GT)], grad.at[pl.ds(g * GT, GT)], sem.at[g])

    def step(g):
        d_copy(2 * g).wait()
        d_copy(2 * g + 1).wait()
        lhs = dv[pl.ds(2 * g, 2)].reshape(256, 256)
        for n in range(8):
            full = nn(lhs, w2[:, 256 * n : 256 * n + 256]).astype(BF)
            for k in range(2):
                for i in range(2):
                    out[(2 * g + k) * GT + 2 * n + i] = full[128 * k : 128 * k + 128, 128 * i : 128 * i + 128]
        copy(2 * g).start()
        copy(2 * g + 1).start()

    loop(0, 8, step)
    loop(0, 16, lambda g: copy(g).wait())
    small[1].wait()
    small[2].wait()


def on_device(atom_feats, atom_counts, w_atom, single_in, w_qkv, w_out, pair, w_pair, cotangent):
    hbm = pl.BlockSpec(memory_space=pl.ANY)
    V = pltpu.VMEM
    dma = pltpu.SemaphoreType.DMA
    wp = w_pair.T
    d_bias, upd, wg = pl.pallas_call(
        main_kernel,
        name="attend",
        out_shape=(
            jax.ShapeDtypeStruct((16, 128, 256), BF),
            jax.ShapeDtypeStruct((16, D), BF),
            jax.ShapeDtypeStruct((16, 128), F32),
        ),
        in_specs=[hbm] * 9,
        out_specs=(hbm, hbm, hbm),
        scratch_shapes=[
            V((256, 128, 128), BF),
            V((256, 128), BF),
            V((16, 128), jnp.int32),
            V((128, D), BF),
            V((16, D), BF),
            V((3, HD, D), BF),
            V((16, 128), BF),
            V((16, 16, D), BF),
            V((16, 16, D), BF),
            V((16, D), F32),
            V((16, 16, D), BF),
            V((16, 16, D), BF),
            V((16, HP, D), BF),
            V((8, 2, 2, HD, 128), BF),
            V((16, 2, HP, 128), BF),
            V((16, HP, 256), BF),
            V((16, HP, 256), BF),
            V((2048, 256), BF),
            V((256, DP), BF),
            V((16, 256, 128), BF),
            V((4, 16, 64, 128), F32),
            V((4, 16, 64, 128), F32),
            V((4, 16, 64, 128), BF),
            V((16, 8, 128), F32),
            V((16, 8, 128), F32),
            V((16, 8, 128), F32),
            V((16, 16, DP), BF),
            V((16, 16, DP), BF),
            V((16, 256, 128), F32),
            V((16, 128, 256), BF),
            V((16, 16, 128), F32),
            V((8, 16, 128), F32),
            V((8, 128, 128), BF),
            V((4, 16, 16, 256), BF),
            V((4, 16, 16, 256), BF),
            V((16, D), BF),
            V((16, D), BF),
            V((16, 128), F32),
            dma((8,)),
            dma((16,)),
            dma((16,)),
            dma((2,)),
        ]
        + [dma((16,))] * 22
        + [dma((8,))] * 4,
        compiler_params=pltpu.CompilerParams(collective_id=0, has_side_effects=True, vmem_limit_bytes=56 << 20),
    )(
        atom_feats,
        atom_counts.reshape(16, 128),
        w_atom,
        single_in,
        jnp.swapaxes(w_qkv, 1, 2),
        w_out,
        pair,
        wp,
        cotangent,
    )
    updated, grad_pair, grad_w = pl.pallas_call(
        grad_kernel,
        name="grad_pair",
        out_shape=(
            jax.ShapeDtypeStruct((16, D), BF),
            jax.ShapeDtypeStruct((256, 128, 128), BF),
            jax.ShapeDtypeStruct((16, 128), F32),
        ),
        in_specs=[hbm] * 4,
        out_specs=(hbm, hbm, hbm),
        scratch_shapes=[
            V((16, 128, 256), BF),
            V((16, 128), BF),
            V((256, 2048), BF),
            V((256, 128, 128), BF),
            dma((3,)),
            dma((16,)),
            dma((16,)),
        ],
        compiler_params=pltpu.CompilerParams(vmem_limit_bytes=60 << 20),
    )(d_bias, wp, upd, wg)
    return updated, grad_pair, grad_w.T


def solution(mesh):
    placed = (
        P(("row", "col"), None),
        P(),
        P(),
        P(("row", "col"), None),
        P(None, None, "col"),
        P("col", None),
        P("row", "col", None),
        P(),
        P(("row", "col"), None),
    )
    return jax.shard_map(
        on_device,
        mesh=mesh,
        in_specs=placed,
        out_specs=(P(("row", "col"), None), P("row", "col", None), P()),
        check_vma=False,
    )
```

time: 353 us -> 75.3 us (0.21)
  blocking collectives: 170 us -> 0 us
  waiting for transfers between devices: 85.7 us -> 0 us
  Pallas kernels: 0 us -> 74.5 us
  matrix products: 25.4 us -> 0 us
  starting transfers between devices: 25.3 us -> 0 us
  other arithmetic: 19.3 us -> 0 us
  between operations: 14.2 us -> 0.64 us
  local copies, waits for them, and re-layouts: 12.2 us -> 0 us
    all_gather x4 -> x0, blocking collectives: 104 us -> none  [the longest x1 31.7 us: on_device(): cot_rows = lax.all_gather(cotangent, 'col', axis=0, tiled=True)]
    reduce_scatter x2 -> x0, waiting for transfers between devices: 85.7 us -> none  [the longest x1 66 us: on_device(): lax.psum_scatter(jnp.dot(attended, w_out, preferred_element_type=jnp.floa...]
    pallas_call x0 -> x2, Pallas kernels: none -> 74.5 us  [the longest x1 68.8 us: on_device(): pl.pallas_call(main_kernel, name='attend', out_shape=(jax.ShapeDtypeStruc...]
    psum x1 -> x0, blocking collectives: 66.3 us -> none  [on_device(): grad_pair_weight = lax.psum(weight_part, ('row', 'col'))]
    dot_general x9 -> x0, matrix products: 25.4 us -> none  [the longest x1 5.66 us: on_device(): jnp.einsum('ijc,ch->hij', pair, w_pair, preferred_element_type=jnp.float32)]
    all_to_all x2 -> x0, starting transfers between devices: 25 us -> none  [the longest x1 16.5 us: on_device(): lax.all_to_all(d_bias, 'col', split_axis=2, concat_axis=0, tiled=True)]
    unnamed x1 -> x0, other arithmetic: 11.6 us -> none
    convert_element_type x3 -> x0, local copies, waits for them, and re-layouts: 7.54 us -> none  [the longest x1 3.75 us: on_device(): d_bias = (probs * (d_probs - inner)).astype(jnp.bfloat16)]
  transfers between devices with their start and end apart: 4 -> 0, of which waited for: 2 -> 0; matrix products, arithmetic and copies ran while one was open for 4% -> 0% of each run, Pallas kernels for 0% -> 0%
where the time goes in v2:
time: 75.3 us; the launch traced here: 75.1 us
  Pallas kernels  74.5 us (99%)
    pallas_call x1, Pallas kernels, on_device(): pl.pallas_call(main_kernel, name='attend', out_shape=(jax.ShapeDtypeStruc...  68.8 us
    pallas_call x1, Pallas kernels, on_device(): pl.pallas_call(grad_kernel, name='grad_pair', out_shape=(jax.ShapeDtypeSt...  5.74 us

profile of v2, /device:TPU:1, one launch (start us, length us, event | category | flops | bytes accessed | tf_op | source)
XLA Modules:
  0.0 75.1 jit_solution(16218393848410571265)
XLA Ops:
  0.6 68.8 %attend.1 = (bf16[16,128,256]{2,1,0:T(8,128)(2,1)}, bf16[16,768]{1,0:T(8,128)(2,1)}, f32[16,128]{1,0:T(8,128)}) custom-call(bf16[160,128]{1,0:T(8,128)(2,1)} %feats.1, s32[16,128]{1,0:T(8,128)} %bitcast.7, bf16[128,768]{1,0:T(8,128)(2,1)} %w_atom.1, bf16[16,768]{1,0:T(8,128)(2,1)} %single_in.1, bf16[3,48,768]{2,1,0:T(8,128)(2,1)} %bitcast.4, ...), custom_call_target="tpu_custom_call" | custom-call | tf_op jit(solution)/shard_map/attend/pallas_call | solution.py:557
  69.4 5.7 %grad_pair.1 = (bf16[16,768]{1,0:T(8,128)(2,1)}, bf16[256,128,128]{2,1,0:T(8,128)(2,1)}, f32[16,128]{1,0:T(8,128)}) custom-call(bf16[16,128,256]{2,1,0:T(8,128)(2,1)} %get-tuple-element.9.d, bf16[16,128]{1,0:T(8,128)(2,1)} %bitcast.6, bf16[16,768]{1,0:T(8,128)(2,1)} %get-tuple-element.10.upd, f32[16,128]{1,0:T(8,128)} %get-tuple-element.11.wg), custom_call_target="tpu_custom_call" | custom-call | tf_op jit(solution)/shard_map/grad_pair/pallas_call | solution.py:625

commit v3 on v2

--- a/solution.py
+++ b/solution.py
@@ -62,11 +62,12 @@
     d_out, upd_out, wg_out,
     pairv, feats_v, counts_v, w_atom_v, single_in_v, wt, wp_v,
     part, pool_recv, acc, norm_all, cot_all, wo_all, kv_row, kv_all, q_all, da_all,
-    wbd, maskp, bias, sbuf, dpbuf, eb, st_send, st_recv, fin_all, att_send, att_recv,
-    dbuf, dt, wcol, wrow, vrow, qrow, darow, single_v, upd_v, wg_v,
+    wbd, maskp, bias, sbuf, dpbuf, eb, st_send, st_recv, st3, mst, cst, fin3, att_send, att_recv,
+    dbuf, dt, wcol, wsum, vrow, qrow, darow, single_v, upd_v,
     in_sem, pair_sem, d_sem, out_sem,
     pool_ss, pool_rs, norm_ss, norm_rs, cot_ss, cot_rs, wo_ss, wo_rs, kv_ss, kv_rs, q_ss, q_rs,
-    da_ss, da_rs, st_ss, st_rs, fin_ss, fin_rs, att_ss, att_rs, wc_ss, wc_rs, kvr_ss, kvr_rs, wr_ss, wr_rs,
+    da_ss, da_rs, st_ss, st_rs, att_ss, att_rs, wc_ss, wc_rs, kvr_ss, kvr_rs, wr_ss, wr_rs, cst_ss, cst_rs,
+    fin_ss, fin_rs, mst_ss, mst_rs,
 ):
     r = lax.axis_index("row")
     c = lax.axis_index("col")
@@ -136,10 +137,21 @@
     da_all[:, HD:HP, :] = pad
     kv_all[:, 0, HD:HP, :] = pad[:, :, 0:128]
     kv_all[:, 1, HD:HP, :] = pad[:, :, 0:128]
+    st_send[...] = jnp.zeros((NC, 8, 128), F32)
     wo_all[:, HD:HP, :] = jnp.zeros((NC, HP - HD, D), BF)
     for n in range(4, 8):
         ins[n].wait()
 
+    def bias_group(k):
+        gs = [2 * k, 2 * k + 1]
+        for g in gs:
+            pair_copy(g).wait()
+        lhs = jnp.concatenate([jnp.concatenate([pairv[g * GT + i] for i in range(GT)], axis=1) for g in gs], axis=0)
+        out = nn(lhs, wbd[...]).astype(BF)
+        for n, g in enumerate(gs):
+            bias[g] = jnp.transpose(out[128 * n : 128 * n + 128])
+
+    loop(0, 1, bias_group)
     pl.semaphore_wait(bar, 22)
 
     def lo(s):
@@ -209,12 +221,7 @@
 
     gather_start(*g_cot)
 
-    def bias_group(g):
-        pair_copy(g).wait()
-        lhs = jnp.concatenate([pairv[g * GT + i] for i in range(GT)], axis=1)
-        bias[g] = jnp.transpose(nn(lhs, wbd[...]).astype(BF))
-
-    loop(0, 3, bias_group)
+    loop(1, 3, bias_group)
 
     acc[...] = single_in_v[...].astype(F32) + part[c].astype(F32)
 
@@ -235,12 +242,12 @@
     gather_start(*g_norm)
 
     gather_relay(*g_cot)
-    loop(3, 6, bias_group)
+    loop(3, 4, bias_group)
     gather_end(*g_cot)
     da_all[c, 0:HD] = nt(wo_all[c, 0:HD], cot_all[...].reshape(256, D)).astype(BF)
     gather_start(*g_da)
 
-    loop(6, 10, bias_group)
+    loop(4, 6, bias_group)
 
     gather_relay(*g_norm)
     gather_end(*g_norm)
@@ -250,12 +257,18 @@
         for n in range(2):
             kv_row[r, half, n] = qkv[HD * (n + 1) : HD * (n + 2), 128 * half : 128 * half + 128]
 
-    def kvr_copy(peer, slot):
-        return pltpu.make_async_remote_copy(
-            kv_row.at[slot], kv_row.at[slot], kvr_ss.at[peer], kvr_rs.at[slot], device_id=(peer, c), device_id_type=MESH
-        )
-
-    loop(1, NR, lambda k: kvr_copy(lax.rem(r + k, NR), r).start())
+    def kvr_copy(peer, slot, half):
+        return pltpu.make_async_remote_copy(
+            kv_row.at[slot, half],
+            kv_row.at[slot, half],
+            kvr_ss.at[2 * peer + half],
+            kvr_rs.at[2 * slot + half],
+            device_id=(peer, c),
+            device_id_type=MESH,
+        )
+
+    for half in range(2):
+        loop(1, NR, lambda k, half=half: kvr_copy(lax.rem(r + k, NR), r, half).start())
     gather_start(*g_q)
 
     def kv_copy(b, half, s):
@@ -268,8 +281,8 @@
             device_id_type=MESH,
         )
 
-    def kv_forward(b):
-        for half in range(2):
+    def kv_forward(b, halves=(0, 1)):
+        for half in halves:
             @pl.when(2 * b + half != c)
             def _(half=half):
                 kv_copy(b, half, c).start()
@@ -279,33 +292,17 @@
                 kv_all[c, :, 0:HD, :] = kv_row[b, half]
 
     kv_forward(r)
+
+    def kvr_take(k, half):
+        b = lax.rem(r + NR - k, NR)
+        kvr_copy(b, b, half).wait_recv()
+        kv_forward(b, (half,))
+
+    for half in range(2):
+        loop(1, NR, lambda k, half=half: kvr_take(k, half))
     gather_relay(*g_da)
-    loop(10, 12, bias_group)
-
-    def kvr_take(k):
-        b = lax.rem(r + NR - k, NR)
-        kvr_copy(b, b).wait_recv()
-        kv_forward(b)
-
-    loop(1, NR, kvr_take)
     gather_relay(*g_q)
-    loop(12, 16, bias_group)
-
-    gather_end(*g_da)
-    dat = jnp.transpose(da_all[...].reshape(DP, 256))
-    for m in range(4):
-        darow[m] = dat[:, 256 * m : 256 * m + 256].reshape(NC, GT, 256)
-    gather_end(*g_q)
-    qt = jnp.transpose(q_all[...].reshape(DP, 256))
-    for m in range(4):
-        qrow[m] = qt[:, 256 * m : 256 * m + 256].reshape(NC, GT, 256)
-
-    def kv_take(h):
-        @pl.when(h != c)
-        def _():
-            kv_copy(0, 0, h).wait_recv()
-
-    loop(0, NC, kv_take)
+    loop(6, 8, bias_group)
 
     lan128 = iota((16, 128), 1)
     first = jnp.where(lan128 < HP, 1.0, 0.0).astype(BF)
@@ -324,7 +321,20 @@
             ]
         return jnp.concatenate(out, axis=0)
 
+    def head_ready(h):
+        @pl.when(h != c)
+        def _():
+            kv_copy(0, 0, h).wait_recv()
+
+        @pl.when(jnp.logical_and(lax.rem(h, 2) != core, h != c))
+        def _():
+            gather_copy(*g_q, mate, h, 0).wait_recv()
+            gather_copy(*g_da, mate, h, 0).wait_recv()
+
     def quad(m):
+        loop(4 * m, 4 * m + 4, head_ready)
+        qrow[m] = jnp.transpose(q_all[4 * m : 4 * m + 4].reshape(256, 256)).reshape(NC, GT, 256)
+        darow[m] = jnp.transpose(da_all[4 * m : 4 * m + 4].reshape(256, 256)).reshape(NC, GT, 256)
         kt = kv_all[4 * m : 4 * m + 4, 0].reshape(4 * HP, 128)
         vt = kv_all[4 * m : 4 * m + 4, 1].reshape(4 * HP, 128)
         sbuf[m] = nn(spread(qrow, m), kt).reshape(NC, 64, 128)
@@ -355,24 +365,28 @@
         t = lane_sum(e * dp)
         e16 = e.astype(BF)
         top = jnp.broadcast_to(top, e.shape)
-        stats = []
-        for u in range(U):
-            part_of = slice(256 * u, 256 * u + 256)
-            rows = to_row(top[part_of]) + to_row(l[part_of]) + to_row(t[part_of]) + [jnp.zeros((2, 128), F32)]
-            stats.append(jnp.concatenate(rows, axis=0))
+        stats = [
+            jnp.concatenate([row for u in range(U) for row in to_row(x[256 * u : 256 * u + 256])], axis=0)
+            for x in (top, l, t)
+        ]
         for u, g in enumerate(gs):
             for m in range(4):
                 k = 256 * u + 64 * m
                 sbuf[m, g] = e[k : k + 64]
                 eb[m, g] = e16[k : k + 64]
-            st_send[g] = stats[u]
-        for g in gs:
-            @pl.when(g != c)
-            def _(g=g):
-                st_copy(g, c).start()
+            st_send[g, 0:2] = stats[0][2 * u : 2 * u + 2]
+        for n in range(3):
+            st3[n, pl.ds(2 * U * q, 2 * U)] = stats[n]
 
     loop(0, NC // U, soft_step)
-    st_recv[c] = st_send[c]
+
+    def half_of(ref, k):
+        return ref.at[:, pl.ds(16 * k, 16)]
+
+    half_copy = pltpu.make_async_remote_copy(
+        half_of(st3, 1 - core), mst, mst_ss, mst_rs, device_id=(r, mate), device_id_type=MESH
+    )
+    half_copy.start()
 
     def att_copy(g, s):
         return pltpu.make_async_remote_copy(
@@ -385,25 +399,113 @@
         full = nn(rows, vrow[p]).reshape(NC, 2, GT, 128)
         att_send[:, :, 128 * p : 128 * p + 128] = jnp.where(keep, full[:, 0], full[:, 1]).astype(BF)
 
-    loop(1, NC, lambda k: st_copy(c, lax.rem(c + NC - k, NC)).wait_recv())
-    sr = st_recv[...]
-    best = jnp.max(sr[:, 0:2, :], axis=0)
-    fac = jnp.exp(sr[:, 0:2, :] - best[None])
-    tot_l = jnp.sum(fac * sr[:, 2:4, :], axis=0)
-    tot_t = jnp.sum(fac * sr[:, 4:6, :], axis=0)
-    inv = 1.0 / tot_l
-    fin_all[c] = jnp.concatenate([best, inv, tot_t * inv, jnp.zeros((2, 128), F32)], axis=0)
-
-    def fin_copy(peer, slot):
-        return pltpu.make_async_remote_copy(
-            fin_all.at[slot], fin_all.at[slot], fin_ss.at[peer], fin_rs.at[slot], device_id=(r, peer), device_id_type=MESH
-        )
-
-    loop(1, NC, lambda k: fin_copy(lax.rem(c + k, NC), c).start())
-    loop(1, NC, lambda k: att_copy(lax.rem(c + k, NC), c).start())
+    half_copy.wait_recv()
+    sa, sb = st3[:, pl.ds(16 * core, 16)], mst[...]
+    top2 = jnp.maximum(sa[0], sb[0])
+    fa, fb = jnp.exp(sa[0] - top2), jnp.exp(sb[0] - top2)
+    cst[chip, 0] = top2
+    cst[chip, 1] = sa[1] * fa + sb[1] * fb
+    cst[chip, 2] = sa[2] * fa + sb[2] * fb
+
+    def cst_copy(peer, slot):
+        return pltpu.make_async_remote_copy(
+            cst.at[slot], cst.at[slot], cst_ss.at[peer], cst_rs.at[slot], device_id=(r, 2 * peer + core), device_id_type=MESH
+        )
+
+    loop(1, 8, lambda k: cst_copy(lax.rem(chip + k, 8), chip).start())
+    def att_start(k):
+        g = lax.rem(c + k, NC)
+        st_copy(g, c).start()
+        att_copy(g, c).start()
+
+    loop(1, NC, att_start)
+    st_recv[c] = st_send[c]
     att_recv[c] = att_send[c]
-
-    frow = fac * inv[None]
+    loop(1, 8, lambda k: cst_copy(chip, lax.rem(chip + 8 - k, 8)).wait_recv())
+    all_st = cst[...]
+    best = jnp.max(all_st[:, 0], axis=0)
+    fac = jnp.exp(all_st[:, 0] - best[None])
+    inv = 1.0 / jnp.sum(fac * all_st[:, 1], axis=0)
+    mine = pl.ds(16 * core, 16)
+    fin3[0, mine] = best
+    fin3[1, mine] = inv
+    fin3[2, mine] = jnp.sum(fac * all_st[:, 2], axis=0) * inv
+
+    def fin_copy(k):
+        return pltpu.make_async_remote_copy(
+            half_of(fin3, k), half_of(fin3, k), fin_ss, fin_rs, device_id=(r, mate), device_id_type=MESH
+        )
+
+    fin_copy(core).start()
+
+
+    def d_copy(g):
+        return pltpu.make_async_copy(dt.at[g], d_out.at[g], d_sem.at[g])
+
+    W = 8
+
+    def d_step(n):
+        k = lax.rem(core + n, 2)
+
+        @pl.when(n == 1)
+        def _():
+            fin_copy(1 - core).wait_recv()
+
+        half = pl.ds(16 * k, 16)
+        scales = jnp.exp(st3[0, half] - fin3[0, half]) * fin3[1, half]
+        inners = fin3[2, half]
+        scale = [to_col(scales[2 * u : 2 * u + 2]) for u in range(W)]
+        inner = [to_col(inners[2 * u : 2 * u + 2]) for u in range(W)]
+        gs = [W * k + u for u in range(W)]
+        e = jnp.concatenate([sbuf[m, g] for g in gs for m in range(4)], axis=0)
+        dp = jnp.concatenate([dpbuf[m, g] for g in gs for m in range(4)], axis=0)
+        d = (e * jnp.concatenate(scale, axis=0)) * (dp - jnp.concatenate(inner, axis=0))
+        dbuf[pl.ds(W * k, W)] = d.reshape(W, 256, 128)
+
+    loop(0, 2, d_step)
+
+    def weight_step(q):
+        lhs = [dbuf[4 * q + n, pl.ds(i, NC, stride=GT), :] for n in range(4) for i in range(GT)]
+        rhs = pairv[pl.ds(4 * GT * q, 4 * GT)].reshape(4 * GT * 128, 128)
+        return nn(jnp.concatenate(lhs, axis=1).astype(BF), rhs)
+
+    wcol[c] = lax.fori_loop(0, 4, lambda q, tot: tot + weight_step(q), jnp.zeros((16, 128), F32))
+
+    def wc_copy(peer, slot):
+        return pltpu.make_async_remote_copy(
+            wcol.at[slot], wcol.at[slot], wc_ss.at[peer], wc_rs.at[slot], device_id=(r, peer), device_id_type=MESH
+        )
+
+    loop(1, NC, lambda k: wc_copy(lax.rem(c + k, NC), c).start())
+
+    gather_relay(*g_wo)
+
+    def d_turn(g):
+        dt[g] = jnp.transpose(dbuf[g].astype(BF))
+        d_copy(g).start()
+
+    loop(0, 16, d_turn)
+
+    loop(1, NC, lambda k: wc_copy(c, lax.rem(c + NC - k, NC)).wait_recv())
+    wsum[...] = jnp.sum(wcol[...], axis=0)
+
+    def wr_copy(peer, slot):
+        return pltpu.make_async_remote_copy(
+            wsum, wg_out.at[slot], wr_ss.at[peer], wr_rs.at[slot], device_id=(peer, c), device_id_type=MESH
+        )
+
+    loop(1, NR, lambda k: wr_copy(lax.rem(r + k, NR), r).start())
+    wg_copy = pltpu.make_async_copy(wsum, wg_out.at[r], out_sem.at[1])
+    wg_copy.start()
+
+    def att_take(k):
+        s = lax.rem(c + NC - k, NC)
+        st_copy(c, s).wait_recv()
+        att_copy(c, s).wait_recv()
+
+    loop(1, NC, att_take)
+    here = pl.ds(2 * c, 2)
+    frow = jnp.exp(st_recv[:, 0:2, :] - fin3[0, here][None]) * fin3[1, here][None]
     fwide = jnp.concatenate([frow[:, 0, :], frow[:, 1, :]], axis=1)
     fbig = jnp.broadcast_to(fwide[:, None, :], (16, 16, 256))
     diag = lax.rem(iota((16, 16, 256), 2), 16) == iota((16, 16, 256), 1)
@@ -411,50 +513,6 @@
     f_hi = fbig.astype(BF)
     f_lo = (fbig - f_hi.astype(F32)).astype(BF)
     f_all = (nn(f_hi, maskp[...]) + nn(f_lo, maskp[...])).reshape(16, 16, DP)
-    gather_relay(*g_wo)
-
-    def d_copy(g):
-        return pltpu.make_async_copy(dt.at[g], d_out.at[g], d_sem.at[g])
-
-    loop(1, NC, lambda k: fin_copy(c, lax.rem(c + NC - k, NC)).wait_recv())
-
-    W = 8
-
-    def d_step(q):
-        gs = [W * q + u for u in range(W)]
-        scale, inner = [], []
-        for g in gs:
-            fin, own = fin_all[g], st_send[g]
-            scale.append(to_col(jnp.exp(own[0:2] - fin[0:2]) * fin[2:4]))
-            inner.append(to_col(fin[4:6]))
-        e = jnp.concatenate([sbuf[m, g] for g in gs for m in range(4)], axis=0)
-        dp = jnp.concatenate([dpbuf[m, g] for g in gs for m in range(4)], axis=0)
-        d = (e * jnp.concatenate(scale, axis=0)) * (dp - jnp.concatenate(inner, axis=0))
-        dbuf[pl.ds(W * q, W)] = d.reshape(W, 256, 128)
-
-    loop(0, NC // W, d_step)
-
-    def weight_step(q):
-        lhs = [dbuf[4 * q + n, pl.ds(i, NC, stride=GT), :] for n in range(4) for i in range(GT)]
-        rhs = pairv[pl.ds(4 * GT * q, 4 * GT)].reshape(4 * GT * 128, 128)
-        return nn(jnp.concatenate(lhs, axis=1).astype(BF), rhs)
-
-    wcol[c] = lax.fori_loop(0, 4, lambda q, tot: tot + weight_step(q), jnp.zeros((16, 128), F32))
-
-    def wc_copy(peer, slot):
-        return pltpu.make_async_remote_copy(
-            wcol.at[slot], wcol.at[slot], wc_ss.at[peer], wc_rs.at[slot], device_id=(r, peer), device_id_type=MESH
-        )
-
-    loop(1, NC, lambda k: wc_copy(lax.rem(c + k, NC), c).start())
-
-    def d_turn(g):
-        dt[g] = jnp.transpose(dbuf[g].astype(BF))
-        d_copy(g).start()
-
-    loop(0, 16, d_turn)
-
-    loop(1, NC, lambda k: att_copy(c, lax.rem(c + NC - k, NC)).wait_recv())
     att = jnp.sum(att_recv[...].astype(F32) * f_all, axis=0).astype(BF)
     gather_end(*g_wo)
     proj = nn(att, wo_all[...].reshape(DP, D))
@@ -462,16 +520,6 @@
     upd_copy = pltpu.make_async_copy(upd_v, upd_out, out_sem.at[0])
     upd_copy.start()
 
-    loop(1, NC, lambda k: wc_copy(c, lax.rem(c + NC - k, NC)).wait_recv())
-    wrow[r] = jnp.sum(wcol[...], axis=0)
-
-    def wr_copy(peer, slot):
-        return pltpu.make_async_remote_copy(
-            wrow.at[slot], wrow.at[slot], wr_ss.at[peer], wr_rs.at[slot], device_id=(peer, c), device_id_type=MESH
-        )
-
-    loop(1, NR, lambda k: wr_copy(lax.rem(r + k, NR), r).start())
-
     def pool_sent(o):
         @pl.when(sends_to(c, o))
         def _():
@@ -480,7 +528,8 @@
     loop(0, NC, pool_sent)
     for g in (g_cot, g_norm, g_da, g_q, g_wo):
         gather_sent(*g)
-    loop(1, NR, lambda k: kvr_copy(lax.rem(r + k, NR), r).wait_send())
+    for half in range(2):
+        loop(1, NR, lambda k, half=half: kvr_copy(lax.rem(r + k, NR), r, half).wait_send())
 
     def kv_sent(b):
         for half in range(2):
@@ -494,25 +543,24 @@
         p = lax.rem(c + k, NC)
         st_copy(p, c).wait_send()
         att_copy(p, c).wait_send()
-        fin_copy(p, c).wait_send()
         wc_copy(p, c).wait_send()
 
     loop(1, NC, col_sent)
+    half_copy.wait_send()
+    fin_copy(core).wait_send()
+    loop(1, 8, lambda k: cst_copy(lax.rem(chip + k, 8), chip).wait_send())
     loop(0, 16, lambda g: d_copy(g).wait())
     upd_copy.wait()
     loop(1, NR, lambda k: wr_copy(r, lax.rem(r + NR - k, NR)).wait_recv())
     loop(1, NR, lambda k: wr_copy(lax.rem(r + k, NR), r).wait_send())
-    wg_v[...] = jnp.sum(wrow[...], axis=0)
-    wg_copy = pltpu.make_async_copy(wg_v, wg_out, out_sem.at[1])
-    wg_copy.start()
     wg_copy.wait()
 
 
-def grad_kernel(d, w_pair, upd, wg, upd_out, grad, wg_out, dv, wp_v, w2, out, in_sem, d_sem, sem):
+def grad_kernel(d, w_pair, upd, wg, upd_out, grad, wg_out, dv, wp_v, wr_v, wg_v, w2, out, in_sem, d_sem, sem):
     small = [
         pltpu.make_async_copy(w_pair, wp_v, in_sem.at[0]),
         pltpu.make_async_copy(upd, upd_out, in_sem.at[1]),
-        pltpu.make_async_copy(wg, wg_out, in_sem.at[2]),
+        pltpu.make_async_copy(wg, wr_v, in_sem.at[2]),
     ]
     for cp in small:
         cp.start()
@@ -544,9 +592,13 @@
         copy(2 * g + 1).start()
 
     loop(0, 8, step)
+    small[2].wait()
+    wg_v[...] = jnp.sum(wr_v[...], axis=0)
+    wg_copy = pltpu.make_async_copy(wg_v, wg_out, in_sem.at[3])
+    wg_copy.start()
     loop(0, 16, lambda g: copy(g).wait())
     small[1].wait()
-    small[2].wait()
+    wg_copy.wait()
 
 
 def on_device(atom_feats, atom_counts, w_atom, single_in, w_qkv, w_out, pair, w_pair, cotangent):
@@ -560,7 +612,7 @@
         out_shape=(
             jax.ShapeDtypeStruct((16, 128, 256), BF),
             jax.ShapeDtypeStruct((16, D), BF),
-            jax.ShapeDtypeStruct((16, 128), F32),
+            jax.ShapeDtypeStruct((NR, 16, 128), F32),
         ),
         in_specs=[hbm] * 9,
         out_specs=(hbm, hbm, hbm),
@@ -590,26 +642,29 @@
             V((4, 16, 64, 128), BF),
             V((16, 8, 128), F32),
             V((16, 8, 128), F32),
-            V((16, 8, 128), F32),
+            V((3, 32, 128), F32),
+            V((3, 16, 128), F32),
+            V((8, 3, 16, 128), F32),
+            V((3, 32, 128), F32),
             V((16, 16, DP), BF),
             V((16, 16, DP), BF),
             V((16, 256, 128), F32),
             V((16, 128, 256), BF),
             V((16, 16, 128), F32),
-            V((8, 16, 128), F32),
+            V((16, 128), F32),
             V((8, 128, 128), BF),
             V((4, 16, 16, 256), BF),
             V((4, 16, 16, 256), BF),
             V((16, D), BF),
             V((16, D), BF),
-            V((16, 128), F32),
             dma((8,)),
             dma((16,)),
             dma((16,)),
             dma((2,)),
         ]
         + [dma((16,))] * 22
-        + [dma((8,))] * 4,
+        + [dma((8,))] * 4
+        + [dma] * 4,
         compiler_params=pltpu.CompilerParams(collective_id=0, has_side_effects=True, vmem_limit_bytes=56 << 20),
     )(
         atom_feats,
@@ -635,9 +690,11 @@
         scratch_shapes=[
             V((16, 128, 256), BF),
             V((16, 128), BF),
+            V((NR, 16, 128), F32),
+            V((16, 128), F32),
             V((256, 2048), BF),
             V((256, 128, 128), BF),
-            dma((3,)),
+            dma((4,)),
             dma((16,)),
             dma((16,)),
         ],

time: 75.3 us -> 69.6 us (0.924)
  Pallas kernels: 74.5 us -> 68.8 us
    pallas_call x1, Pallas kernels: 68.8 us -> 63 us  [on_device(): pl.pallas_call(main_kernel, name='attend', out_shape=(jax.ShapeDtypeStruc...]
where the time goes in v3:
time: 69.6 us; the launch traced here: 69.4 us
  Pallas kernels  68.8 us (99%)
    pallas_call x1, Pallas kernels, on_device(): pl.pallas_call(main_kernel, name='attend', out_shape=(jax.ShapeDtypeStruc...  63 us
    pallas_call x1, Pallas kernels, on_device(): pl.pallas_call(grad_kernel, name='grad_pair', out_shape=(jax.ShapeDtypeSt...  5.75 us

profile of v3, /device:TPU:1, one launch (start us, length us, event | category | flops | bytes accessed | tf_op | source)
XLA Modules:
  0.0 69.4 jit_solution(5029144084561735042)
XLA Ops:
  0.6 63.0 %attend.1 = (bf16[16,128,256]{2,1,0:T(8,128)(2,1)}, bf16[16,768]{1,0:T(8,128)(2,1)}, f32[8,16,128]{2,1,0:T(8,128)}) custom-call(bf16[160,128]{1,0:T(8,128)(2,1)} %feats.1, s32[16,128]{1,0:T(8,128)} %bitcast.7, bf16[128,768]{1,0:T(8,128)(2,1)} %w_atom.1, bf16[16,768]{1,0:T(8,128)(2,1)} %single_in.1, bf16[3,48,768]{2,1,0:T(8,128)(2,1)} %bitcast.4, ...), custom_call_target="tpu_custom_call" | custom-call | tf_op jit(solution)/shard_map/attend/pallas_call | solution.py:609
  63.7 5.7 %grad_pair.1 = (bf16[16,768]{1,0:T(8,128)(2,1)}, bf16[256,128,128]{2,1,0:T(8,128)(2,1)}, f32[16,128]{1,0:T(8,128)}) custom-call(bf16[16,128,256]{2,1,0:T(8,128)(2,1)} %get-tuple-element.9.d, bf16[16,128]{1,0:T(8,128)(2,1)} %bitcast.6, bf16[16,768]{1,0:T(8,128)(2,1)} %get-tuple-element.10.upd, f32[8,16,128]{2,1,0:T(8,128)} %get-tuple-element.11.wg), custom_call_target="tpu_custom_call" | custom-call | tf_op jit(solution)/shard_map/grad_pair/pallas_call | solution.py:680

commit v4 on v3

--- a/solution.py
+++ b/solution.py
@@ -378,7 +378,7 @@
         for n in range(3):
             st3[n, pl.ds(2 * U * q, 2 * U)] = stats[n]
 
-    loop(0, NC // U, soft_step)
+    loop(0, 2, lambda n: soft_step(2 * (1 - core) + n))
 
     def half_of(ref, k):
         return ref.at[:, pl.ds(16 * k, 16)]
@@ -387,17 +387,12 @@
         half_of(st3, 1 - core), mst, mst_ss, mst_rs, device_id=(r, mate), device_id_type=MESH
     )
     half_copy.start()
+    loop(0, 2, lambda n: soft_step(2 * core + n))
 
     def att_copy(g, s):
         return pltpu.make_async_remote_copy(
             att_send.at[g], att_recv.at[s], att_ss.at[g], att_rs.at[s], device_id=(r, g), device_id_type=MESH
         )
-
-    keep = iota((16, 16, 128), 2) < HP
-    for p in range(8):
-        rows = eb[p // 2, :, 32 * (p % 2) : 32 * (p % 2) + 32, :].reshape(512, 128)
-        full = nn(rows, vrow[p]).reshape(NC, 2, GT, 128)
-        att_send[:, :, 128 * p : 128 * p + 128] = jnp.where(keep, full[:, 0], full[:, 1]).astype(BF)
 
     half_copy.wait_recv()
     sa, sb = st3[:, pl.ds(16 * core, 16)], mst[...]
@@ -413,6 +408,12 @@
         )
 
     loop(1, 8, lambda k: cst_copy(lax.rem(chip + k, 8), chip).start())
+    keep = iota((16, 16, 128), 2) < HP
+    for p in range(8):
+        rows = eb[p // 2, :, 32 * (p % 2) : 32 * (p % 2) + 32, :].reshape(512, 128)
+        full = nn(rows, vrow[p]).reshape(NC, 2, GT, 128)
+        att_send[:, :, 128 * p : 128 * p + 128] = jnp.where(keep, full[:, 0], full[:, 1]).astype(BF)
+
     def att_start(k):
         g = lax.rem(c + k, NC)
         st_copy(g, c).start()

time: 69.6 us -> 69.6 us (level)
  no operation moved by 1% of the time
where the time goes in v4:
time: 69.6 us; the launch traced here: 69.4 us
  Pallas kernels  68.8 us (99%)
    pallas_call x1, Pallas kernels, on_device(): pl.pallas_call(main_kernel, name='attend', out_shape=(jax.ShapeDtypeStruc...  63 us
    pallas_call x1, Pallas kernels, on_device(): pl.pallas_call(grad_kernel, name='grad_pair', out_shape=(jax.ShapeDtypeSt...  5.75 us

profile of v4, /device:TPU:1, one launch (start us, length us, event | category | flops | bytes accessed | tf_op | source)
XLA Modules:
  0.0 69.4 jit_solution(7004355985219344213)
XLA Ops:
  0.6 63.0 %attend.1 = (bf16[16,128,256]{2,1,0:T(8,128)(2,1)}, bf16[16,768]{1,0:T(8,128)(2,1)}, f32[8,16,128]{2,1,0:T(8,128)}) custom-call(bf16[160,128]{1,0:T(8,128)(2,1)} %feats.1, s32[16,128]{1,0:T(8,128)} %bitcast.7, bf16[128,768]{1,0:T(8,128)(2,1)} %w_atom.1, bf16[16,768]{1,0:T(8,128)(2,1)} %single_in.1, bf16[3,48,768]{2,1,0:T(8,128)(2,1)} %bitcast.4, ...), custom_call_target="tpu_custom_call" | custom-call | tf_op jit(solution)/shard_map/attend/pallas_call | solution.py:610
  63.7 5.7 %grad_pair.1 = (bf16[16,768]{1,0:T(8,128)(2,1)}, bf16[256,128,128]{2,1,0:T(8,128)(2,1)}, f32[16,128]{1,0:T(8,128)}) custom-call(bf16[16,128,256]{2,1,0:T(8,128)(2,1)} %get-tuple-element.9.d, bf16[16,128]{1,0:T(8,128)(2,1)} %bitcast.6, bf16[16,768]{1,0:T(8,128)(2,1)} %get-tuple-element.10.upd, f32[8,16,128]{2,1,0:T(8,128)} %get-tuple-element.11.wg), custom_call_target="tpu_custom_call" | custom-call | tf_op jit(solution)/shard_map/grad_pair/pallas_call | solution.py:681
